TPU v7x, 32 devices: a whole 2x2x4 slice. The times are simulated.
32 devices in a mesh: tiles: 8 (over z, y), chan: 4 (over x, core).
Axes of the slice: x: 2, y: 2, z: 4, core: 2. Of those that a mesh axis runs over, the one named last changes fastest.
Arguments:
- x_scan: bfloat16 [128, 192, 256], P('tiles', 'chan'), may hold values from -40 to 40
- slot_owner: int32 [128], P('tiles'), may hold values from 0 to 64, as said below
- adjacency: int32 [64, 8], P('tiles'), may hold values from 0 to 64, as said below
- cotangent: bfloat16 [64, 192, 256], P('tiles', 'chan'), may hold values from -6 to 6
- dw_weight: float32 [192, 49], P('chan'), may hold values from -0.875 to 0.875
- ln_gain: bfloat16 [192], P('chan'), may hold values from 0.25 to 1.75
- w_in: bfloat16 [192, 768], P(None, 'chan'), may hold values from -0.4375 to 0.4375
- b_in: bfloat16 [768], P('chan'), may hold values from -3 to 3
- w_out: bfloat16 [768, 192], P('chan'), may hold values from -0.21875 to 0.21875
- layer_scale: float32 [192], P('chan'), may hold values from 0.3 to 1.5
Outputs:
- output: bfloat16 [64, 192, 256], P('tiles', 'chan')
- grad_in: bfloat16 [64, 192, 256], P('tiles', 'chan')
- grad_dw: float32 [192, 49], P('chan')
- grad_w1: float32 [192, 768], P(None, 'chan')
- grad_w2: float32 [768, 192], P('chan')
Inputs may be any that keep to these rules, and one draw needn't show every extreme that they name: `slot_owner`: slots run in scan order over a grid of tiles with 16 columns, one grid row for each device along tiles. A tissue slot holds its tile's owner-order index, a background slot holds 64. Tissue tiles are numbered in scan order, and owner-order index q belongs to device q // 8. Grid rows 2k and 2k + 1 hold 4 to 12 tissue tiles each and 16 together, so a device's tissue tiles belong to it or to the device whose index differs in the lowest bit, and at most 4 of them, a number reached in every draw, to the latter. `adjacency`: entry k of a tissue tile is the owner-order index of the grid cell at row and column offsets (-1,-1), (-1,0), (-1,1), (0,-1), (0,1), (1,-1), (1,0), (1,1) from it, 64 where that cell is background or off the grid. Every neighbour of a tile owned by device o is owned by one of the devices o - 3 to o + 3, a distance reached in every draw.
All inputs are finite; a program needn't handle non-finite values.
Results may differ from a plain program's by a relative error of at most 0.015.
Values may be sent and summed in bfloat16 or wider, within the bound.
A program may use at most 128 MiB of HBM per device.

v0:
```python
import math

import jax
import jax.numpy as jnp
from jax import lax
from jax.sharding import PartitionSpec as P

CHANNEL_COUNT = 192
P_SIZE = 16
REACH = 3
PIX = 256


EPSILON = 1e-06
GELU_SCALE = 0.7978845608
GELU_CUBIC = 0.044715


def from_partner(value, axis, distance):
    return lax.ppermute(value, axis, [(i, i ^ 1 << distance) for i in range(lax.axis_size(axis))])


def passed_along(value, axis, by):
    length = lax.axis_size(axis)
    pairs = [(i, i + by) for i in range(length) if 0 <= i + by < length]
    return lax.ppermute(value, axis, pairs)


def strips(tile_field):
    side_len = tile_field.shape[-1]
    top_rows = tile_field[:, :, :3, :]
    bottom_rows = tile_field[:, :, side_len - 3 :, :]
    left_cols = jnp.swapaxes(tile_field[:, :, :, :3], 2, 3)
    right_cols = jnp.swapaxes(tile_field[:, :, :, side_len - 3 :], 2, 3)
    return jnp.stack([top_rows, bottom_rows, left_cols, right_cols], axis=2)


def assemble(tile_field, around):
    side_len = tile_field.shape[-1]
    upper_band = jnp.concatenate(
        [around[:, 0, :, 1, :, side_len - 3 :], around[:, 1, :, 1], around[:, 2, :, 1, :, :3]],
        axis=3,
    )
    middle = jnp.concatenate(
        [
            jnp.swapaxes(around[:, 3, :, 3], 2, 3),
            tile_field,
            jnp.swapaxes(around[:, 4, :, 2], 2, 3),
        ],
        axis=3,
    )
    lower_band = jnp.concatenate(
        [around[:, 5, :, 0, :, side_len - 3 :], around[:, 6, :, 0], around[:, 7, :, 0, :, :3]],
        axis=3,
    )
    return jnp.concatenate([upper_band, middle, lower_band], axis=2)


def depthwise(padded, kernel):
    tile_count = padded.shape[0]
    channels = padded.shape[1]
    wide_len = padded.shape[3]
    side_len = wide_len - 6
    span_len = side_len * wide_len
    flat_pad = jnp.pad(
        padded.astype(jnp.float32).reshape(tile_count, channels, wide_len * wide_len),
        ((0, 0), (0, 0), (0, 8)),
    )
    result = jnp.zeros((tile_count, channels, span_len), jnp.float32)
    for row_tap in range(7):
        for col_tap in range(7):
            offset = row_tap * wide_len + col_tap
            result = (
                result
                + kernel[:, row_tap * 7 + col_tap][None, :, None]
                * flat_pad[:, :, offset : offset + span_len]
            )
    return result.reshape(tile_count, channels, side_len, wide_len)[:, :, :, :side_len]


def kernel_grad(grad_tiles, padded):
    tile_count = grad_tiles.shape[0]
    channels = grad_tiles.shape[1]
    side_len = grad_tiles.shape[3]
    wide_len = side_len + 6
    span_len = side_len * wide_len
    flat_pad = jnp.pad(
        padded.astype(jnp.float32).reshape(tile_count, channels, wide_len * wide_len),
        ((0, 0), (0, 0), (0, 8)),
    )
    spread = jnp.pad(grad_tiles.astype(jnp.float32), ((0, 0), (0, 0), (0, 0), (0, 6))).reshape(
        tile_count, channels, span_len
    )
    columns = []
    for row_tap in range(7):
        for col_tap in range(7):
            offset = row_tap * wide_len + col_tap
            columns.append(
                jnp.sum(spread * flat_pad[:, :, offset : offset + span_len], axis=(0, 2))
            )
    return jnp.stack(columns, axis=1)


def gelu_parts(preact):
    tanh_arg = GELU_SCALE * (preact + GELU_CUBIC * preact * preact * preact)
    tangent = jnp.tanh(tanh_arg)
    values = 0.5 * preact * (1.0 + tangent)
    slopes = 0.5 * (1.0 + tangent) + 0.5 * preact * (1.0 - tangent * tangent) * GELU_SCALE * (
        1.0 + 3.0 * GELU_CUBIC * preact * preact
    )
    return (values, slopes)


def relay_tiles(x_scan, slot_owner, tile_count):
    my_index = lax.axis_index("tiles")
    partner = jnp.bitwise_xor(my_index, 1)
    owner_dev = slot_owner // tile_count
    position = slot_owner % tile_count
    slot_rows = x_scan.reshape(x_scan.shape[0], x_scan.shape[1] * x_scan.shape[2])
    targets = jnp.arange(tile_count, dtype=jnp.int32)
    staying = owner_dev == my_index
    keep_map = ((position[None, :] == targets[:, None]) & staying[None, :]).astype(jnp.bfloat16)
    kept_rows = jnp.dot(keep_map, slot_rows, preferred_element_type=jnp.float32)
    leaving = owner_dev == partner
    leave_rank = jnp.cumsum(leaving.astype(jnp.int32)) - 1
    outgoing = (
        leave_rank[None, :] == jnp.arange(tile_count // 2, dtype=jnp.int32)[:, None]
    ) & leaving[None, :]
    sent_rows = jnp.dot(
        outgoing.astype(jnp.bfloat16), slot_rows, preferred_element_type=jnp.float32
    ).astype(jnp.bfloat16)
    filled = jnp.any(outgoing, axis=1)
    sent_place = jnp.where(
        filled, jnp.sum(jnp.where(outgoing, position[None, :], 0), axis=1), tile_count
    )
    arrived_rows, arrived_place = from_partner((sent_rows, sent_place), "tiles", 0)
    settle_map = (arrived_place[None, :] == targets[:, None]).astype(jnp.bfloat16)
    merged = kept_rows + jnp.dot(settle_map, arrived_rows, preferred_element_type=jnp.float32)
    return merged.astype(jnp.bfloat16).reshape(tile_count, x_scan.shape[1], x_scan.shape[2])


def neighbour_rims(tile_field, adjacency, tile_count):
    rims = strips(tile_field)
    rim_shape = rims.shape
    rim_rows = rims.reshape(rim_shape[0], rim_shape[1] * rim_shape[2] * rim_shape[3] * rim_shape[4])
    pieces = []
    for offset in range(-REACH, REACH + 1):
        if offset == 0:
            pieces.append(rim_rows)
        else:
            pieces.append(passed_along(rim_rows, "tiles", -offset))
    rim_table = jnp.concatenate(pieces, axis=0)
    my_index = lax.axis_index("tiles")
    local_ids = adjacency - (my_index - REACH) * tile_count
    valid = (
        (adjacency < tile_count * lax.axis_size("tiles"))
        & (local_ids >= 0)
        & (local_ids < rim_table.shape[0])
    )
    found = jnp.take(rim_table, jnp.clip(local_ids, 0, rim_table.shape[0] - 1), axis=0)
    found = jnp.where(valid[:, :, None], found, jnp.zeros((), found.dtype))
    return found.reshape(rim_shape[0], 8, rim_shape[1], rim_shape[2], rim_shape[3], rim_shape[4])


def body(
    x_scan, slot_owner, adjacency, cotangent, dw_weight, ln_gain, w_in, b_in, w_out, layer_scale
):
    tile_count = adjacency.shape[0]
    channels = x_scan.shape[1]
    owned_tiles = relay_tiles(x_scan, slot_owner, tile_count)
    tile_field = owned_tiles.reshape(tile_count, channels, P_SIZE, P_SIZE)
    padded = assemble(tile_field, neighbour_rims(tile_field, adjacency, tile_count))
    mixed_tiles = (
        depthwise(padded, dw_weight).astype(jnp.bfloat16).reshape(tile_count, channels, PIX)
    )
    scale_col = layer_scale[None, :, None]
    mixed_f = mixed_tiles.astype(jnp.float32)
    moments = lax.psum((jnp.sum(mixed_f, axis=1), jnp.sum(mixed_f * mixed_f, axis=1)), "chan")
    row_mean = moments[0] / CHANNEL_COUNT
    inverse_deviation = lax.rsqrt(moments[1] / CHANNEL_COUNT - row_mean * row_mean + EPSILON)
    centered_input = (mixed_f - row_mean[:, None, :]) * inverse_deviation[:, None, :]
    gain_float = ln_gain.astype(jnp.float32)
    normed = (centered_input * gain_float[None, :, None]).astype(jnp.bfloat16)
    all_normed = lax.all_gather(normed, "chan", axis=1, tiled=True)
    preact = (
        jnp.einsum("tcp,ch->thp", all_normed, w_in, preferred_element_type=jnp.float32)
        + b_in.astype(jnp.float32)[None, :, None]
    )
    values, slopes = gelu_parts(preact)
    activated = values.astype(jnp.bfloat16)
    partial_out = jnp.einsum("thp,hc->tcp", activated, w_out, preferred_element_type=jnp.float32)
    branch = lax.psum_scatter(
        partial_out.astype(jnp.bfloat16), "chan", scatter_dimension=1, tiled=True
    )
    output = (owned_tiles.astype(jnp.float32) + scale_col * branch.astype(jnp.float32)).astype(
        jnp.bfloat16
    )
    dbranch = (cotangent.astype(jnp.float32) * scale_col).astype(jnp.bfloat16)
    all_dbranch = lax.all_gather(dbranch, "chan", axis=1, tiled=True)
    act_grad = jnp.einsum("tcp,hc->thp", all_dbranch, w_out, preferred_element_type=jnp.float32)
    pre_grad = (act_grad * slopes).astype(jnp.bfloat16)
    raw_w2 = jnp.einsum("thp,tcp->hc", activated, all_dbranch, preferred_element_type=jnp.float32)
    raw_w1 = jnp.einsum("tcp,thp->ch", all_normed, pre_grad, preferred_element_type=jnp.float32)
    partial_in = jnp.einsum("thp,ch->tcp", pre_grad, w_in, preferred_element_type=jnp.float32)
    normed_gradient = lax.psum_scatter(
        partial_in.astype(jnp.bfloat16), "chan", scatter_dimension=1, tiled=True
    ).astype(jnp.float32)
    centered_input_gradient = normed_gradient * gain_float[None, :, None]
    gradient_moments = lax.psum(
        (
            jnp.sum(centered_input_gradient, axis=1),
            jnp.sum(centered_input_gradient * centered_input, axis=1),
        ),
        "chan",
    )
    mixed_gradient = (
        inverse_deviation[:, None, :]
        * (
            centered_input_gradient
            - gradient_moments[0][:, None, :] / CHANNEL_COUNT
            - centered_input * gradient_moments[1][:, None, :] / CHANNEL_COUNT
        )
    ).astype(jnp.bfloat16)
    grad_field = mixed_gradient.reshape(tile_count, channels, P_SIZE, P_SIZE)
    dpadded = assemble(grad_field, neighbour_rims(grad_field, adjacency, tile_count))
    backflow = depthwise(dpadded, dw_weight[:, ::-1]).reshape(tile_count, channels, PIX)
    grad_in = (cotangent.astype(jnp.float32) + backflow).astype(jnp.bfloat16)
    local_dw = kernel_grad(grad_field, padded)
    totals = lax.psum((local_dw, raw_w1, raw_w2), "tiles")
    factor = 1.0 / math.sqrt(tile_count * lax.axis_size("tiles") * PIX)
    return (output, grad_in, totals[0] * factor, totals[1] * factor, totals[2] * factor)


def solution(mesh):
    in_specs = (
        P("tiles", "chan", None),
        P("tiles"),
        P("tiles", None),
        P("tiles", "chan", None),
        P("chan", None),
        P("chan"),
        P(None, "chan"),
        P("chan"),
        P("chan", None),
        P("chan"),
    )
    out_specs = (
        P("tiles", "chan", None),
        P("tiles", "chan", None),
        P("chan", None),
        P(None, "chan"),
        P("chan", None),
    )
    return jax.shard_map(body, mesh=mesh, in_specs=in_specs, out_specs=out_specs, check_vma=False)
```

profile of v0, /device:TPU:0, one launch (start us, length us, event | category | flops | bytes accessed | tf_op | source)
XLA Modules:
  0.0 415.0 jit_solution(6966639543029558465)
XLA Ops:
  9.1 3.0 collective-permute-start
  16.6 1.5 collective-permute-done.1
  20.8 1.9 slice_bitcast_fusion.1
  22.7 4.3 %copy.189 = bf16[8,48,3,16]{2,3,1,0:T(8,128)(2,1)} copy(bf16[8,48,3,16]{3,2,1,0:T(4,128)(2,1)} %get-tuple-element.160) | data formatting | bytes 73728
  27.0 4.2 %copy.190 = bf16[8,48,3,16]{2,3,1,0:T(8,128)(2,1)} copy(bf16[8,48,3,16]{3,2,1,0:T(4,128)(2,1)} %get-tuple-element.161) | data formatting | bytes 73728
  31.2 6.4 %pad_maximum_fusion = bf16[8,48,4,3,16]{3,4,1,0,2:T(8,128)(2,1)} fusion(bf16[8,48,1,3,16]{3,4,1,0,2:T(8,128)(2,1)} %get-tuple-element.163, bf16[8,48,1,3,16]{3,4,1,0,2:T(8,128)(2,1)S(1)} %get-tuple-element.162, bf16[8,48,1,3,16]{3,4,1,0,2:T(8,128)(2,1)} %bitcast.323, bf16[8,48,1,3,16]{3,4,1,0,2:T(8,128)(2,1)} %bitcast.322), kind=kLoop, calls=%fused_computation.5 | loop fusion | flops 221184 | bytes 294912 | tf_op jit(solution)/shard_map/stack | solution.py:35
  37.6 10.7 %copy.145 = bf16[8,48,4,3,16]{4,3,2,1,0:T(4,128)(2,1)S(1)} copy(bf16[8,48,4,3,16]{3,4,1,0,2:T(8,128)(2,1)} %pad_maximum_fusion) | data formatting | bytes 294912 | tf_op jit(solution)/shard_map/stack | solution.py:35
  48.3 2.0 reshape.207
  50.3 3.6 collective-permute-start.2
  60.1 5.0 %collective-permute-start.4 = (bf16[8,9216]{1,0:T(8,128)(2,1)}, bf16[8,9216]{1,0:T(8,128)(2,1)S(1)}, u32[]{:S(2)}, u32[]{:S(2)}) collective-permute-start(bf16[8,9216]{1,0:T(8,128)(2,1)} %reshape.207), channel_id=1, source_target_pairs={{0,4},{4,8},{8,12},{12,16},{16,20},{20,24},{24,28},{1,5},{5,9},{9,... | collective-permute-start | bytes 442376 | tf_op jit(solution)/shard_map/ppermute | solution.py:26
  65.1 4.9 %collective-permute-start.3 = (bf16[8,9216]{1,0:T(8,128)(2,1)}, bf16[8,9216]{1,0:T(8,128)(2,1)S(1)}, u32[]{:S(2)}, u32[]{:S(2)}) collective-permute-start(bf16[8,9216]{1,0:T(8,128)(2,1)} %reshape.207), channel_id=1, source_target_pairs={{0,8},{4,12},{8,16},{12,20},{16,24},{20,28},{1,9},{5,13},{9,17},{1... | collective-permute-start | bytes 442376 | tf_op jit(solution)/shard_map/ppermute | solution.py:26
  70.1 2.8 collective-permute-done.3
  73.0 2.3 gather_fusion
  75.3 1.5 fusion.114
  76.8 13.5 %reshape.208 = bf16[8,8,48,4,3,16]{5,4,3,2,1,0:T(4,128)(2,1)} reshape(bf16[8,8,9216]{2,1,0:T(8,128)(2,1)S(1)} %fusion.114) | data formatting | bytes 2359296 | tf_op jit(solution)/shard_map/reshape | solution.py:162
  90.3 3.0 slice_bitcast_fusion.6
  93.4 2.9 slice_bitcast_fusion.7
  101.2 4.2 %copy.191 = bf16[8,1,48,1,3,16]{4,5,2,0,3,1:T(8,128)(2,1)} copy(bf16[8,1,48,1,3,16]{5,4,3,2,1,0:T(4,128)(2,1)} %get-tuple-element.157) | data formatting | bytes 73728
  105.4 3.3 copy.192
  108.7 3.3 pad_maximum_fusion.1
  112.1 1.6 copy.154
  115.0 11.1 %add_convert_fusion = bf16[8,48,352]{1,0,2:T(8,128)(2,1)S(1)} fusion(f32[8,48,484]{1,0,2:T(8,128)S(1)} %bitcast_convert_fusion.1, f32[48]{0:T(128)S(1)} %copy-done.56, f32[48]{0:T(128)S(1)} %copy-done.58, f32[48]{0:T(128)S(1)} %get-tuple-element.85, f32[48]{0:T(128)S(1)} %get-tuple-element.86, f32[48]{0:T(128)S(1)} %get-tuple-element.87, ...), kind=kLoop, calls=%fused_computation.228 | loop fusion | flops 13246464 | bytes 64272704 | tf_op jit(solution)/shard_map/convert.9
  128.0 1.6 copy.157
  129.6 10.4 %all-reduce.5 = (f32[8,256]{1,0:T(8,128)S(1)}, f32[8,256]{1,0:T(8,128)S(1)}) all-reduce(f32[8,256]{1,0:T(8,128)S(1)} %copy.158, f32[8,256]{1,0:T(8,128)S(1)} %copy.156), channel_id=1, replica_groups=mesh['tiles'=8,'chan'=4] {'chan'}, use_global_device_ids=true, to_apply=%region_6.8 | all-reduce | flops 4096 | bytes 32768 | tf_op jit(solution)/shard_map/psum | solution.py:178
  140.0 8.8 %all_gather.6 = bf16[8,192,256]{2,1,0:T(8,128)(2,1)S(1)} all-gather(bf16[8,48,256]{2,1,0:T(8,128)(2,1)S(1)} %multiply_convert_fusion.2), channel_id=1, replica_groups=mesh['tiles'=8,'chan'=4] {'chan'}, dimensions={1}, use_global_device_ids=true | all-gather | bytes 983040 | tf_op jit(solution)/shard_map/all_gather | solution.py:184
  151.3 1.6 fusion.111
  153.8 25.0 %reduce-scatter.3.cloned.1.call-done = bf16[8,48,256]{2,1,0:T(8,128)(2,1)} async-done(((bf16[8,192,256]{2,1,0:T(8,128)(2,1)}), bf16[8,48,256]{2,1,0:T(8,128)(2,1)}) %reduce-scatter.3.cloned.1.call-update) | async-done | bytes 196624 | tf_op jit(solution)/shard_map/reduce_scatter | solution.py:192
  178.8 2.2 fusion.116
  181.0 8.2 %all_gather.7 = bf16[8,192,256]{2,1,0:T(8,128)(2,1)S(1)} all-gather(bf16[8,48,256]{2,1,0:T(8,128)(2,1)S(1)} %get-tuple-element.171), channel_id=1, replica_groups=mesh['tiles'=8,'chan'=4] {'chan'}, dimensions={1}, use_global_device_ids=true | all-gather | bytes 983040 | tf_op jit(solution)/shard_map/all_gather | solution.py:199
  189.2 1.3 convolution_bitcast_fusion
  193.7 2.4 fusion.112
  196.1 69.5 %all-reduce.8.cloned.1.call-done = (f32[192,192]{1,0:T(8,128)}, f32[192,192]{1,0:T(8,128)}) async-done(((f32[192,192]{1,0:T(8,128)}, f32[192,192]{1,0:T(8,128)}), (f32[192,192]{1,0:T(8,128)}, f32[192,192]{1,0:T(8,128)})) %all-reduce.8.cloned.1.call-update) | async-done | bytes 294928 | tf_op jit(solution)/shard_map/psum | solution.py:229
  265.7 1.8 broadcast_multiply_fusion
  267.4 23.1 %reduce-scatter.5.cloned.1.call-done = bf16[8,48,256]{2,1,0:T(8,128)(2,1)} async-done(((bf16[8,192,256]{2,1,0:T(8,128)(2,1)}), bf16[8,48,256]{2,1,0:T(8,128)(2,1)}) %reduce-scatter.5.cloned.1.call-update) | async-done | bytes 196624 | tf_op jit(solution)/shard_map/reduce_scatter | solution.py:205
  291.6 10.1 %all-reduce.4 = (f32[8,256]{1,0:T(8,128)S(1)}, f32[8,256]{1,0:T(8,128)S(1)}) all-reduce(f32[8,256]{1,0:T(8,128)S(1)} %get-tuple-element.83, f32[8,256]{1,0:T(8,128)S(1)} %get-tuple-element.82), channel_id=1, replica_groups=mesh['tiles'=8,'chan'=4] {'chan'}, use_global_device_ids=true, to_apply=%region_12.14 | all-reduce | flops 4096 | bytes 32768 | tf_op jit(solution)/shard_map/psum | solution.py:209
  305.7 2.2 fusion.108
  307.9 2.8 fusion.109
  310.7 2.8 fusion.110
  314.1 2.3 copy.165
  321.7 4.6 %collective-permute-start.10 = (bf16[8,9216]{1,0:T(8,128)(2,1)S(1)}, bf16[8,9216]{1,0:T(8,128)(2,1)S(1)}, u32[]{:S(2)}, u32[]{:S(2)}) collective-permute-start(bf16[8,9216]{1,0:T(8,128)(2,1)S(1)} %reshape.211), channel_id=1, source_target_pairs={{0,4},{4,8},{8,12},{12,16},{16,20},{20,24},{24,28},{1,5},{5,9},{9,... | collective-permute-start | bytes 442376 | tf_op jit(solution)/shard_map/ppermute | solution.py:26
  326.2 7.0 %collective-permute-start.8 = (bf16[8,9216]{1,0:T(8,128)(2,1)S(1)}, bf16[8,9216]{1,0:T(8,128)(2,1)S(1)}, u32[]{:S(2)}, u32[]{:S(2)}) collective-permute-start(bf16[8,9216]{1,0:T(8,128)(2,1)S(1)} %reshape.211), channel_id=1, source_target_pairs={{0,12},{4,16},{8,20},{12,24},{16,28},{1,13},{5,17},{9,21},{13,25},... | collective-permute-start | bytes 442376 | tf_op jit(solution)/shard_map/ppermute | solution.py:26
  333.4 34.5 %psum.53 = f32[48,49]{0,1:T(8,128)S(1)} all-reduce(f32[48,49]{0,1:T(8,128)S(1)} %stack.239), channel_id=1, replica_groups=mesh['tiles'=8,'chan'=4] {'tiles'}, use_global_device_ids=true, to_apply=%region_62.64 | all-reduce | flops 2352 | bytes 18816 | tf_op jit(solution)/shard_map/psum | solution.py:229
  368.6 1.5 collective-permute-start.9
  370.1 2.4 collective-permute-done.9
  374.2 13.5 %reshape.212 = bf16[8,8,48,4,3,16]{5,4,3,2,1,0:T(4,128)(2,1)} reshape(bf16[8,8,9216]{2,1,0:T(8,128)(2,1)S(1)} %fusion.113) | data formatting | bytes 2359296 | tf_op jit(solution)/shard_map/reshape | solution.py:162
  387.7 2.0 fusion.134
  389.7 2.1 fusion.133
  395.4 11.0 %fusion.14 = f32[8,48,352]{1,0,2:T(8,128)S(1)} fusion(f32[8,48,484]{1,0,2:T(8,128)S(1)} %bitcast_convert_fusion, f32[48]{0:T(128)S(1)} %copy-done.57, f32[48]{0:T(128)S(1)} %copy-done.59, f32[48]{0:T(128)S(1)} %get-tuple-element.85, f32[48]{0:T(128)S(1)} %get-tuple-element.86, f32[48]{0:T(128)S(1)} %get-tuple-element.87, f32[48]{0:T(128)S(1)} %copy-done.13, ...), kind=kLoop, calls=%fused_computation.39 | loop fusion | flops 13111296 | bytes 64544960 | tf_op jit(solution)/shard_map/add | solution.py:74
  (301 shorter events, 47.5 us)
Async XLA Ops:
  7.2 144.1 %copy-start = (bf16[192,192]{1,0:T(8,128)(2,1)S(1)}, bf16[192,192]{1,0:T(8,128)(2,1)}, u32[]{:S(2)}) copy-start(bf16[192,192]{1,0:T(8,128)(2,1)} %param.20) | copy-start | bytes 221188
  7.2 7.1 %copy-start.2 = (f32[48,49]{1,0:T(8,128)S(1)}, f32[48,49]{1,0:T(8,128)}, u32[]{:S(2)}) copy-start(f32[48,49]{1,0:T(8,128)} %param.16) | copy-start | bytes 28228
  7.2 171.6 %reduce-scatter.3.cloned.1.call-start = ((), (), s32[]{:S(2)}) async-start(), calls=%async_computation.2 | async-start | bytes 983040 | tf_op jit(solution)/shard_map/reduce_scatter | solution.py:192
  9.1 7.6 %collective-permute-start = (s32[4]{0:T(128)S(1)}, s32[4]{0:T(128)S(1)}, u32[]{:S(2)}, u32[]{:S(2)}) collective-permute-start(s32[4]{0:T(128)S(1)} %broadcast_select_fusion), channel_id=1, source_target_pairs={{0,4},{4,0},{8,12},{12,8},{16,20},{20,16},{24,28},{28,24},{1,5},{5... | collective-permute-start | bytes 56 | tf_op jit(solution)/shard_map/ppermute | solution.py:20
  13.4 4.7 %collective-permute-start.1 = (bf16[4,12288]{1,0:T(4,128)(2,1)S(1)}, bf16[4,12288]{1,0:T(4,128)(2,1)S(1)}, u32[]{:S(2)}, u32[]{:S(2)}) collective-permute-start(bf16[4,12288]{1,0:T(4,128)(2,1)S(1)} %convolution_convert_fusion), channel_id=1, source_target_pairs={{0,4},{4,0},{8,12},{12,8},{16,20},{20,16},{24,28},{28,24},{1,5},{5... | collective-permute-start | bytes 294920 | tf_op jit(solution)/shard_map/ppermute | solution.py:20
  48.3 5.7 %copy-start.94 = (bf16[48]{0:T(256)(128)(2,1)S(1)}, bf16[48]{0:T(256)(128)(2,1)}, u32[]{:S(2)}) copy-start(bf16[48]{0:T(256)(128)(2,1)} %param.17) | copy-start | bytes 292
  48.3 6.2 %copy-start.95 = (bf16[192]{0:T(256)(128)(2,1)S(1)}, bf16[192]{0:T(256)(128)(2,1)}, u32[]{:S(2)}) copy-start(bf16[192]{0:T(256)(128)(2,1)} %param.19) | copy-start | bytes 1156
  50.3 22.6 %copy-start.9 = (bf16[8,9216]{1,0:T(8,128)(2,1)S(1)}, bf16[8,9216]{1,0:T(8,128)(2,1)}, u32[]{:S(2)}) copy-start(bf16[8,9216]{1,0:T(8,128)(2,1)} %reshape.207) | copy-start | bytes 442372
  50.3 14.8 %collective-permute-start.2 = (bf16[8,9216]{1,0:T(8,128)(2,1)}, bf16[8,9216]{1,0:T(8,128)(2,1)S(1)}, u32[]{:S(2)}, u32[]{:S(2)}) collective-permute-start(bf16[8,9216]{1,0:T(8,128)(2,1)} %reshape.207), channel_id=1, source_target_pairs={{0,12},{4,16},{8,20},{12,24},{16,28},{1,13},{5,17},{9,21},{13,25},... | collective-permute-start | bytes 442376 | tf_op jit(solution)/shard_map/ppermute | solution.py:26
  56.2 58.4 %copy-start.60 = (f32[48]{0:T(128)}, f32[48]{0:T(128)S(1)}, u32[]{:S(2)}) copy-start(f32[48]{0:T(128)S(1)} %get-tuple-element.103) | copy-start | bytes 580
  56.2 16.8 %collective-permute-start.7 = (bf16[8,9216]{1,0:T(8,128)(2,1)}, bf16[8,9216]{1,0:T(8,128)(2,1)S(1)}, u32[]{:S(2)}, u32[]{:S(2)}) collective-permute-start(bf16[8,9216]{1,0:T(8,128)(2,1)} %reshape.207), channel_id=1, source_target_pairs={{12,0},{16,4},{20,8},{24,12},{28,16},{13,1},{17,5},{21,9},{25,13},... | collective-permute-start | bytes 442376 | tf_op jit(solution)/shard_map/ppermute | solution.py:26
  57.5 15.5 %collective-permute-start.6 = (bf16[8,9216]{1,0:T(8,128)(2,1)}, bf16[8,9216]{1,0:T(8,128)(2,1)S(1)}, u32[]{:S(2)}, u32[]{:S(2)}) collective-permute-start(bf16[8,9216]{1,0:T(8,128)(2,1)} %reshape.207), channel_id=1, source_target_pairs={{8,0},{12,4},{16,8},{20,12},{24,16},{28,20},{9,1},{13,5},{17,9},{2... | collective-permute-start | bytes 442376 | tf_op jit(solution)/shard_map/ppermute | solution.py:26
  58.8 14.1 %collective-permute-start.5 = (bf16[8,9216]{1,0:T(8,128)(2,1)}, bf16[8,9216]{1,0:T(8,128)(2,1)S(1)}, u32[]{:S(2)}, u32[]{:S(2)}) collective-permute-start(bf16[8,9216]{1,0:T(8,128)(2,1)} %reshape.207), channel_id=1, source_target_pairs={{4,0},{8,4},{12,8},{16,12},{20,16},{24,20},{28,24},{5,1},{9,5},{13... | collective-permute-start | bytes 442376 | tf_op jit(solution)/shard_map/ppermute | solution.py:26
  60.1 12.8 %collective-permute-start.4 = (bf16[8,9216]{1,0:T(8,128)(2,1)}, bf16[8,9216]{1,0:T(8,128)(2,1)S(1)}, u32[]{:S(2)}, u32[]{:S(2)}) collective-permute-start(bf16[8,9216]{1,0:T(8,128)(2,1)} %reshape.207), channel_id=1, source_target_pairs={{0,4},{4,8},{8,12},{12,16},{16,20},{20,24},{24,28},{1,5},{5,9},{9,... | collective-permute-start | bytes 442376 | tf_op jit(solution)/shard_map/ppermute | solution.py:26
  65.1 7.7 %collective-permute-start.3 = (bf16[8,9216]{1,0:T(8,128)(2,1)}, bf16[8,9216]{1,0:T(8,128)(2,1)S(1)}, u32[]{:S(2)}, u32[]{:S(2)}) collective-permute-start(bf16[8,9216]{1,0:T(8,128)(2,1)} %reshape.207), channel_id=1, source_target_pairs={{0,8},{4,12},{8,16},{12,20},{16,24},{20,28},{1,9},{5,13},{9,17},{1... | collective-permute-start | bytes 442376 | tf_op jit(solution)/shard_map/ppermute | solution.py:26
  100.0 5.4 %copy-start.7 = (bf16[8,1,48,1,3,16]{5,4,3,2,1,0:T(4,128)(2,1)S(1)}, bf16[8,1,48,1,3,16]{5,4,3,2,1,0:T(4,128)(2,1)}, u32[]{:S(2)}) copy-start(bf16[8,1,48,1,3,16]{5,4,3,2,1,0:T(4,128)(2,1)} %get-tuple-element.159) | copy-start | bytes 110596
  112.0 1.7 copy-start.11
  112.1 1.7 copy-start.12
  114.0 0.7 copy-start.17
  114.0 0.7 copy-start.20
  114.1 0.7 copy-start.32
  114.3 0.7 copy-start.64
  114.3 0.7 copy-start.80
  126.8 13.2 %copy-start.90 = (f32[48]{0:T(128)S(1)}, f32[48]{0:T(128)}, u32[]{:S(2)}) copy-start(f32[48]{0:T(128)} %convert_element_type.107) | copy-start | bytes 580
  128.0 20.8 %copy-start.92 = (f32[192]{0:T(256)S(1)}, f32[192]{0:T(256)}, u32[]{:S(2)}) copy-start(f32[192]{0:T(256)} %convert_element_type.109) | copy-start | bytes 2308
  150.2 1.2 copy-start.5
  151.3 27.5 %copy-start.93 = (f32[48]{0:T(128)S(1)}, f32[48]{0:T(128)}, u32[]{:S(2)}) copy-start(f32[48]{0:T(128)} %param.21) | copy-start | bytes 580
  153.0 112.7 %all-reduce.8.cloned.1.call-start = ((), (), s32[]{:S(2)}) async-start(), calls=%async_computation.4 | async-start | bytes 786432 | tf_op jit(solution)/shard_map/psum | solution.py:229
  178.8 10.4 %copy-start.6 = (f32[8,256,192]{1,2,0:T(8,128)S(1)}, f32[8,256,192]{1,2,0:T(8,128)}, u32[]{:S(2)}) copy-start(f32[8,256,192]{1,2,0:T(8,128)} %copy-done.5) | copy-start | bytes 4718596
  191.7 0.9 copy-start.3
  192.6 1.1 copy-start.10
  193.7 96.9 %reduce-scatter.5.cloned.1.call-start = ((), (), s32[]{:S(2)}) async-start(), calls=%async_computation.3 | async-start | bytes 983040 | tf_op jit(solution)/shard_map/reduce_scatter | solution.py:205
  196.1 105.7 %copy-start.91 = (f32[48]{0:T(128)S(1)}, f32[48]{0:T(128)}, u32[]{:S(2)}) copy-start(f32[48]{0:T(128)} %convert_element_type.107) | copy-start | bytes 580
  317.8 54.9 %collective-permute-start.13 = (bf16[8,9216]{1,0:T(8,128)(2,1)S(1)}, bf16[8,9216]{1,0:T(8,128)(2,1)S(1)}, u32[]{:S(2)}, u32[]{:S(2)}) collective-permute-start(bf16[8,9216]{1,0:T(8,128)(2,1)S(1)} %reshape.211), channel_id=1, source_target_pairs={{12,0},{16,4},{20,8},{24,12},{28,16},{13,1},{17,5},{21,9},{25,13},... | collective-permute-start | bytes 442376 | tf_op jit(solution)/shard_map/ppermute | solution.py:26
  319.1 53.5 %collective-permute-start.12 = (bf16[8,9216]{1,0:T(8,128)(2,1)S(1)}, bf16[8,9216]{1,0:T(8,128)(2,1)S(1)}, u32[]{:S(2)}, u32[]{:S(2)}) collective-permute-start(bf16[8,9216]{1,0:T(8,128)(2,1)S(1)} %reshape.211), channel_id=1, source_target_pairs={{8,0},{12,4},{16,8},{20,12},{24,16},{28,20},{9,1},{13,5},{17,9},{2... | collective-permute-start | bytes 442376 | tf_op jit(solution)/shard_map/ppermute | solution.py:26
  320.4 52.2 %collective-permute-start.11 = (bf16[8,9216]{1,0:T(8,128)(2,1)S(1)}, bf16[8,9216]{1,0:T(8,128)(2,1)S(1)}, u32[]{:S(2)}, u32[]{:S(2)}) collective-permute-start(bf16[8,9216]{1,0:T(8,128)(2,1)S(1)} %reshape.211), channel_id=1, source_target_pairs={{4,0},{8,4},{12,8},{16,12},{20,16},{24,20},{28,24},{5,1},{9,5},{13... | collective-permute-start | bytes 442376 | tf_op jit(solution)/shard_map/ppermute | solution.py:26
  321.7 50.9 %collective-permute-start.10 = (bf16[8,9216]{1,0:T(8,128)(2,1)S(1)}, bf16[8,9216]{1,0:T(8,128)(2,1)S(1)}, u32[]{:S(2)}, u32[]{:S(2)}) collective-permute-start(bf16[8,9216]{1,0:T(8,128)(2,1)S(1)} %reshape.211), channel_id=1, source_target_pairs={{0,4},{4,8},{8,12},{12,16},{16,20},{20,24},{24,28},{1,5},{5,9},{9,... | collective-permute-start | bytes 442376 | tf_op jit(solution)/shard_map/ppermute | solution.py:26
  326.2 42.3 %collective-permute-start.8 = (bf16[8,9216]{1,0:T(8,128)(2,1)S(1)}, bf16[8,9216]{1,0:T(8,128)(2,1)S(1)}, u32[]{:S(2)}, u32[]{:S(2)}) collective-permute-start(bf16[8,9216]{1,0:T(8,128)(2,1)S(1)} %reshape.211), channel_id=1, source_target_pairs={{0,12},{4,16},{8,20},{12,24},{16,28},{1,13},{5,17},{9,21},{13,25},... | collective-permute-start | bytes 442376 | tf_op jit(solution)/shard_map/ppermute | solution.py:26
  368.6 3.9 collective-permute-start.9
  392.4 1.6 copy-start.4
  394.4 0.7 copy-start.21
  394.4 0.7 copy-start.33
  394.6 0.7 copy-start.65
  394.7 0.7 copy-start.81
  394.7 0.7 copy-start.86
  394.7 0.7 copy-start.88
  406.4 0.9 copy-start.8
  406.4 1.6 copy-start.1
  (65 other events, 43.3 us)
Sparse Core Ops, SparseCore 0:
  153.1 25.6 reduce-scatter.2
  193.8 71.8 all-reduce.7
  268.2 22.3 reduce-scatter.4
where the time goes:
time: 422 us; the launch traced here: 415 us
  waiting for transfers between devices  124 us (29%)
  local copies, waits for them, and re-layouts  100 us (24%)
  blocking collectives  72 us (17%)
  other arithmetic  55.9 us (13%)
  starting transfers between devices  37.6 us (9%)
  between operations  15.6 us (4%)
  matrix products  9.38 us (2%)
    psum x1, waiting for transfers between devices, body(): totals = lax.psum((local_dw, raw_w1, raw_w2), 'tiles')  69.5 us
    psum x1, blocking collectives, body(): totals = lax.psum((local_dw, raw_w1, raw_w2), 'tiles')  34.5 us
    ppermute x12, starting transfers between devices, passed_along(): return lax.ppermute(value, axis, pairs)  34.3 us
    reshape x2, local copies, waits for them, and re-layouts, neighbour_rims(): found.reshape(rim_shape[0], 8, rim_shape[1], rim_shape[2], rim_shape[3],...  27.1 us
    reduce_scatter x1, waiting for transfers between devices, body(): lax.psum_scatter(partial_out.astype(jnp.bfloat16), 'chan', scatter_dimens...  25 us
    unnamed x218, local copies, waits for them, and re-layouts  23.7 us
    reduce_scatter x1, waiting for transfers between devices, body(): lax.psum_scatter(partial_in.astype(jnp.bfloat16), 'chan', scatter_dimensi...  23.1 us
    another operation x5, local copies, waits for them, and re-layouts, strips(): return jnp.stack([top_rows, bottom_rows, left_cols, right_cols], axis=2)  15.2 us
  transfers between devices with their start and end apart: 17, of which 6 were waited for; matrix products, arithmetic and copies ran while one was open for 3% of the time, Pallas kernels for 0%

commit v1 on v0

v1 whole, which is shorter than its diff:
```python
import math

import jax
import jax.numpy as jnp
import numpy as np
from jax import lax
from jax.experimental import pallas as pl
from jax.experimental.pallas import tpu as pltpu
from jax.sharding import PartitionSpec as P

CHANNEL_COUNT = 192
PIX = 256
REACH = 3
WIDE = 24
PAD_ROWS = 544
SHIFT_ROWS = 528

EPSILON = 1e-06
GELU_SCALE = 0.7978845608
GELU_CUBIC = 0.044715

F32 = jnp.float32
BF16 = jnp.bfloat16
NT = (((1,), (1,)), ((), ()))


def placement():
    m = np.zeros((PAD_ROWS, 4 * PIX), np.float32)
    for i in range(22):
        for j in range(22):
            ii, jj = (i - 3) % 16, (j - 3) % 16
            inner_i, inner_j = 3 <= i < 19, 3 <= j < 19
            if inner_i and inner_j:
                part = 3
            elif inner_j:
                part = 0
            elif inner_i:
                part = 1
            else:
                part = 2
            m[i * WIDE + j, part * PIX + ii * 16 + jj] = 1.0
    return m


def fill_padded(ids, table, place, joined, pad):
    lane = lax.broadcasted_iota(jnp.int32, (48, PIX), 1)
    low = lane >= 128
    right = (lane % 16) >= 8

    def one(t, carry):
        def at(k):
            return table[ids[t, k]].astype(F32)

        rows = pl.ds(pl.multiple_of(t * 48, 48), 48)
        joined[rows, 0:PIX] = jnp.where(low, at(1), at(6)).astype(BF16)
        joined[rows, PIX : 2 * PIX] = jnp.where(right, at(3), at(4)).astype(BF16)
        joined[rows, 2 * PIX : 3 * PIX] = jnp.where(
            low, jnp.where(right, at(0), at(2)), jnp.where(right, at(5), at(7))
        ).astype(BF16)
        joined[rows, 3 * PIX : 4 * PIX] = table[REACH * 8 + t]
        return carry

    lax.fori_loop(0, 8, one, 0)
    pad[...] = lax.dot_general(place[...], joined[...], NT, preferred_element_type=F32)


def shift_copies(pad, shifted):
    for b in range(7):
        shifted[b] = pad[b : b + SHIFT_ROWS, :]


def convolve(shifted, weights, result):
    def row(i, carry):
        acc = jnp.zeros((16, 384), F32)
        for a in range(7):
            start = pl.multiple_of((i + a) * WIDE, 8)
            for b in range(7):
                tap = a * 7 + b
                acc = acc + weights[tap : tap + 1, :] * shifted[b, pl.ds(start, 16), :]
        result[pl.ds(pl.multiple_of(i * 16, 16), 16), :] = acc
        return carry

    lax.fori_loop(0, 16, row, 0)


def load_table(pieces, table):
    for o in range(7):
        table[o * 8 : o * 8 + 8] = pieces[o][...]
    table[56] = jnp.zeros((48, PIX), BF16)


def forward_conv(ids, p0, p1, p2, p3, p4, p5, p6, place, weights, mixed, padded,
                 table, joined, pad, shifted, result):
    load_table((p0, p1, p2, p3, p4, p5, p6), table)
    fill_padded(ids, table, place, joined, pad)
    padded[...] = pad[...].astype(BF16)
    shift_copies(pad, shifted)
    convolve(shifted, weights, result)
    mixed[...] = result[...].T.astype(BF16)


def backward_conv(ids, p0, p1, p2, p3, p4, p5, p6, place, weights, padded, cotangent, fold,
                  grad_in, grad_dw, table, joined, pad, shifted, result, taps):
    load_table((p0, p1, p2, p3, p4, p5, p6), table)
    fill_padded(ids, table, place, joined, pad)
    shift_copies(pad, shifted)
    convolve(shifted, weights, result)
    grad_in[...] = (cotangent[...].astype(F32) + result[...].T).astype(BF16)

    def keep(i, carry):
        start = pl.multiple_of((i + 3) * WIDE, 8)
        result[pl.ds(pl.multiple_of(i * 16, 16), 16), :] = shifted[3, pl.ds(start, 16), :]
        return carry

    lax.fori_loop(0, 16, keep, 0)
    pad[...] = padded[...].astype(F32)
    shift_copies(pad, shifted)
    for a in range(7):

        def row(i, sums):
            start = pl.multiple_of((i + a) * WIDE, 8)
            grad = result[pl.ds(pl.multiple_of(i * 16, 16), 16), :]
            new = []
            for b in range(7):
                prod = grad * shifted[b, pl.ds(start, 16), :]
                new.append(sums[b] + prod[0:8] + prod[8:16])
            return tuple(new)

        sums = lax.fori_loop(0, 16, row, tuple(jnp.zeros((8, 384), F32) for _ in range(7)))
        for b in range(7):
            tap = a * 7 + b
            taps[tap : tap + 1, :] = jnp.sum(sums[b], axis=0, keepdims=True)
    taps[49:56, :] = jnp.zeros((7, 384), F32)
    grad_dw[...] = jnp.dot(
        taps[...], fold[...], precision=lax.Precision.HIGHEST, preferred_element_type=F32
    )


def mlp(perm, m0, m1, m2, m3, d0, d1, d2, d3, wi, wit, wo, wot, bias,
        part_out, part_in, raw, stats, sum1, sum2):
    ms, ds = (m0, m1, m2, m3), (d0, d1, d2, d3)
    gain = jnp.concatenate([d[8].astype(F32) for d in ds], axis=0)
    sum1[...] = jnp.zeros_like(sum1)
    sum2[...] = jnp.zeros_like(sum2)
    for k in range(4):
        part_in[k, 8] = jnp.zeros((48, PIX), BF16)
    s1_all, s2_all = [], []
    for t in range(8):
        mixed = jnp.concatenate([m[t].astype(F32) for m in ms], axis=0)
        mean = jnp.sum(mixed, axis=0, keepdims=True) * (1.0 / CHANNEL_COUNT)
        square = jnp.sum(mixed * mixed, axis=0, keepdims=True) * (1.0 / CHANNEL_COUNT)
        inv = lax.rsqrt(square - mean * mean + EPSILON)
        xhat = (mixed - mean) * inv
        stats[0, t : t + 1, :] = mean
        stats[1, t : t + 1, :] = inv
        normed = (xhat * gain).astype(BF16)
        dbranch = jnp.concatenate([d[t] for d in ds], axis=0)
        pre = jnp.dot(wit[...], normed, preferred_element_type=F32) + bias[...]
        tangent = jnp.tanh(GELU_SCALE * (pre + GELU_CUBIC * pre * pre * pre))
        act = (0.5 * pre * (1.0 + tangent)).astype(BF16)
        slope = 0.5 * (1.0 + tangent) + 0.5 * pre * (1.0 - tangent * tangent) * GELU_SCALE * (
            1.0 + 3.0 * GELU_CUBIC * pre * pre
        )
        out = jnp.dot(wot[...], act, preferred_element_type=F32).astype(BF16)
        act_grad = jnp.dot(wo[...], dbranch, preferred_element_type=F32)
        pre_grad = (act_grad * slope).astype(BF16)
        back = jnp.dot(wi[...], pre_grad, preferred_element_type=F32).astype(BF16)
        sum1[...] += lax.dot_general(normed, pre_grad, NT, preferred_element_type=F32)
        sum2[...] += lax.dot_general(dbranch, act, NT, preferred_element_type=F32)
        for k in range(4):
            part_out[k, t] = out[k * 48 : k * 48 + 48]
            part_in[k, t] = back[k * 48 : k * 48 + 48]
        xgrad = back.astype(F32) * gain
        s1_all.append(jnp.sum(xgrad, axis=0, keepdims=True))
        s2_all.append(jnp.sum(xgrad * xhat, axis=0, keepdims=True))
    rows = []
    for total in (jnp.concatenate(s1_all, axis=0), jnp.concatenate(s2_all, axis=0)):
        high = total.astype(BF16).astype(F32)
        rows.append(high)
        rows.append(total - high)
    packed = jnp.concatenate(rows, axis=0).astype(BF16)
    for k in range(4):
        part_in[k, 8, 0:32, :] = packed
        raw[perm[k]] = sum1[k * 48 : k * 48 + 48, :].astype(BF16)
        raw[4 + perm[k]] = sum2[k * 48 : k * 48 + 48, :].astype(BF16)


VM = pl.BlockSpec(memory_space=pltpu.VMEM)
SM = pl.BlockSpec(memory_space=pltpu.SMEM)
PARAMS = pltpu.CompilerParams(vmem_limit_bytes=40 * 1024 * 1024)


def conv_scratch():
    return [
        pltpu.VMEM((57, 48, PIX), BF16),
        pltpu.VMEM((384, 4 * PIX), BF16),
        pltpu.VMEM((PAD_ROWS, 384), F32),
        pltpu.VMEM((7, SHIFT_ROWS, 384), F32),
        pltpu.VMEM((PIX, 384), F32),
    ]


def xor_pass(value, axis, bit):
    return lax.ppermute(value, axis, [(i, i ^ bit) for i in range(lax.axis_size(axis))])


def passed_along(value, axis, by):
    length = lax.axis_size(axis)
    pairs = [(i, i + by) for i in range(length) if 0 <= i + by < length]
    return lax.ppermute(value, axis, pairs)


def around(tiles):
    return [
        tiles if offset == 0 else passed_along(tiles, "tiles", -offset)
        for offset in range(-REACH, REACH + 1)
    ]


def relay_tiles(x_scan, slot_owner, tile_count):
    my_index = lax.axis_index("tiles")
    partner = jnp.bitwise_xor(my_index, 1)
    owner_dev = slot_owner // tile_count
    position = slot_owner % tile_count
    slots = jnp.arange(x_scan.shape[0], dtype=jnp.int32)
    targets = jnp.arange(tile_count, dtype=jnp.int32)
    half = tile_count // 2
    leaving = owner_dev == partner
    rank = jnp.cumsum(leaving.astype(jnp.int32)) - 1
    outgoing = (rank[None, :] == targets[:half, None]) & leaving[None, :]
    pick = jnp.sum(jnp.where(outgoing, slots[None, :], 0), axis=1)
    place = jnp.where(
        jnp.any(outgoing, axis=1),
        jnp.sum(jnp.where(outgoing, position[None, :], 0), axis=1),
        tile_count,
    )
    sent = jnp.take(x_scan, pick, axis=0, mode="clip")
    arrived, arrived_place = xor_pass((sent, place), "tiles", 1)
    staying = (position[None, :] == targets[:, None]) & (owner_dev == my_index)[None, :]
    source = jnp.sum(jnp.where(staying, slots[None, :], 0), axis=1)
    landed = arrived_place[None, :] == targets[:, None]
    ranks = targets[:half]
    source = source + jnp.sum(
        jnp.where(landed, x_scan.shape[0] + ranks[None, :], 0), axis=1
    )
    return jnp.take(jnp.concatenate([x_scan, arrived], axis=0), source, axis=0, mode="clip")


def body(
    x_scan, slot_owner, adjacency, cotangent, dw_weight, ln_gain, w_in, b_in, w_out, layer_scale
):
    tile_count = adjacency.shape[0]
    n_tiles = lax.axis_size("tiles")
    channels = x_scan.shape[1]
    rows = tile_count * channels
    me_t, me_c = lax.axis_index("tiles"), lax.axis_index("chan")
    scale_col = layer_scale[None, :, None]
    gain_float = ln_gain.astype(F32)[None, :, None]

    dbranch = (cotangent.astype(F32) * scale_col).astype(BF16)
    ext = jnp.concatenate(
        [dbranch, jnp.broadcast_to(ln_gain[None, :, None], (1, channels, PIX))], axis=0
    )
    d_all = [ext] + [xor_pass(ext, "chan", k) for k in (1, 2, 3)]

    perm = jnp.bitwise_xor(jnp.arange(4, dtype=jnp.int32), me_c)
    wi = jnp.take(w_in.reshape(4, channels, -1), perm, axis=0, mode="clip").reshape(w_in.shape)
    wot = jnp.take(w_out.T.reshape(4, channels, -1), perm, axis=0, mode="clip")
    wot = wot.reshape(CHANNEL_COUNT, -1)
    taps = jnp.tile(dw_weight.T, (1, tile_count))
    taps_back = jnp.tile(dw_weight[:, ::-1].T, (1, tile_count))
    place = jnp.asarray(placement(), BF16)
    fold = jnp.asarray(np.tile(np.eye(channels, dtype=np.float32), (tile_count, 1)))
    local_ids = adjacency - (me_t - REACH) * tile_count
    valid = (
        (adjacency < tile_count * n_tiles)
        & (local_ids >= 0)
        & (local_ids < (2 * REACH + 1) * tile_count)
    )
    ids = jnp.where(valid, local_ids, (2 * REACH + 1) * tile_count)

    owned = relay_tiles(x_scan, slot_owner, tile_count)
    mixed, padded = pl.pallas_call(
        forward_conv,
        out_shape=(
            jax.ShapeDtypeStruct((rows, PIX), BF16),
            jax.ShapeDtypeStruct((PAD_ROWS, rows), BF16),
        ),
        in_specs=[SM] + [VM] * 9,
        out_specs=(VM, VM),
        scratch_shapes=conv_scratch(),
        compiler_params=PARAMS,
        name="forward_conv",
    )(ids, *around(owned), place, taps)
    mixed = mixed.reshape(tile_count, channels, PIX)
    m_all = [mixed] + [xor_pass(mixed, "chan", k) for k in (1, 2, 3)]

    hidden = w_in.shape[1]
    part_out, part_in, raw, stats = pl.pallas_call(
        mlp,
        out_shape=(
            jax.ShapeDtypeStruct((4, tile_count, channels, PIX), BF16),
            jax.ShapeDtypeStruct((4, tile_count + 1, channels, PIX), BF16),
            jax.ShapeDtypeStruct((8, channels, hidden), BF16),
            jax.ShapeDtypeStruct((2, tile_count, PIX), F32),
        ),
        in_specs=[SM] + [VM] * 13,
        out_specs=(VM,) * 4,
        scratch_shapes=[pltpu.VMEM((CHANNEL_COUNT, hidden), F32)] * 2,
        compiler_params=PARAMS,
        name="mlp",
    )(perm, *m_all, *d_all, wi, wi.T, wot.T, wot, b_in.astype(F32)[:, None])

    back = [part_in[0]] + [xor_pass(part_in[k], "chan", k) for k in (1, 2, 3)]
    total = sum(b.astype(F32) for b in back[1:]) + back[0].astype(F32)
    dnormed = total[:tile_count]
    extra = total[tile_count]
    grad_sum = (extra[0:8] + extra[8:16]) / CHANNEL_COUNT
    grad_dot = (extra[16:24] + extra[24:32]) / CHANNEL_COUNT
    inv = stats[1][:, None, :]
    xhat = (mixed.astype(F32) - stats[0][:, None, :]) * inv
    dmixed = (
        inv * (dnormed * gain_float - grad_sum[:, None, :] - xhat * grad_dot[:, None, :])
    ).astype(BF16)

    pieces = around(dmixed)

    fwd = [part_out[0]] + [xor_pass(part_out[k], "chan", k) for k in (1, 2, 3)]
    branch = sum(b.astype(F32) for b in fwd[1:]) + fwd[0].astype(F32)
    branch = branch.astype(BF16).astype(F32)
    output = (owned.astype(F32) + scale_col * branch).astype(BF16)

    weights_sum = raw
    steps = [1 << s for s in range(n_tiles.bit_length() - 1)]
    for bit in steps:
        other = xor_pass(weights_sum, "tiles", bit)
        exact = weights_sum.astype(F32) + other.astype(F32)
        if bit != steps[-1]:
            exact = lax.reduce_precision(exact, 8, 7)
            weights_sum = exact.astype(BF16)
    factor = 1.0 / math.sqrt(tile_count * n_tiles * PIX)
    grad_w1 = exact[:4].reshape(CHANNEL_COUNT, hidden) * factor
    grad_w2 = (exact[4:].reshape(CHANNEL_COUNT, hidden) * factor).T

    grad_in, grad_dw = pl.pallas_call(
        backward_conv,
        out_shape=(
            jax.ShapeDtypeStruct((rows, PIX), BF16),
            jax.ShapeDtypeStruct((56, channels), F32),
        ),
        in_specs=[SM] + [VM] * 12,
        out_specs=(VM, VM),
        scratch_shapes=conv_scratch() + [pltpu.VMEM((56, rows), F32)],
        compiler_params=PARAMS,
        name="backward_conv",
    )(ids, *pieces, place, taps_back, padded, cotangent.reshape(rows, PIX), fold)
    for bit in steps:
        grad_dw = grad_dw + xor_pass(grad_dw, "tiles", bit)
    grad_dw = grad_dw[:49].T * factor
    return (output, grad_in.reshape(tile_count, channels, PIX), grad_dw, grad_w1, grad_w2)


def solution(mesh):
    in_specs = (
        P("tiles", "chan", None),
        P("tiles"),
        P("tiles", None),
        P("tiles", "chan", None),
        P("chan", None),
        P("chan"),
        P(None, "chan"),
        P("chan"),
        P("chan", None),
        P("chan"),
    )
    out_specs = (
        P("tiles", "chan", None),
        P("tiles", "chan", None),
        P("chan", None),
        P(None, "chan"),
        P("chan", None),
    )
    return jax.shard_map(body, mesh=mesh, in_specs=in_specs, out_specs=out_specs, check_vma=False)
```

time: 422 us -> 135 us (0.32); the launches traced: 415 us -> 134 us
  local copies, waits for them, and re-layouts: 100 us -> 9.15 us
  waiting for transfers between devices: 124 us -> 51.6 us
  blocking collectives: 72 us -> 0 us
  other arithmetic: 55.9 us -> 6.17 us
  Pallas kernels: 0 us -> 17.9 us
  between operations: 15.6 us -> 1.24 us
  starting transfers between devices: 37.6 us -> 48.2 us
  matrix products: 9.38 us -> 0 us
    psum x1 -> x0, waiting for transfers between devices: 69.5 us -> none  [body(): totals = lax.psum((local_dw, raw_w1, raw_w2), 'tiles')]
    psum x3 -> x0, blocking collectives: 55 us -> none  [the longest x1 34.5 us: body(): totals = lax.psum((local_dw, raw_w1, raw_w2), 'tiles')]
    reduce_scatter x2 -> x0, waiting for transfers between devices: 48.1 us -> none  [the longest x1 25 us: body(): lax.psum_scatter(partial_out.astype(jnp.bfloat16), 'chan', scatter_dimens...]
    reshape x8 -> x1, local copies, waits for them, and re-layouts: 32.9 us -> 0.1 us  [body(): jnp.take(w_in.reshape(4, channels, -1), perm, axis=0, mode='clip')]
    ppermute x2 -> x20, waiting for transfers between devices: 1.46 us -> 29.5 us  [xor_pass(): lax.ppermute(value, axis, [(i, i ^ bit) for i in range(lax.axis_size(axis...]
    unnamed x218 -> x26, local copies, waits for them, and re-layouts: 23.7 us -> 2.45 us
    ppermute x2 -> x20, starting transfers between devices: 3.11 us -> 23.2 us  [xor_pass(): lax.ppermute(value, axis, [(i, i ^ bit) for i in range(lax.axis_size(axis...]
    another operation x5 -> x2, other arithmetic: 18.7 us -> 0.04 us
  transfers between devices with their start and end apart: 17 -> 32, of which waited for: 6 -> 16; matrix products, arithmetic and copies ran while one was open for 3% -> 7% of each run, Pallas kernels for 0% -> 10%
where the time goes in v1:
time: 135 us; the launch traced here: 134 us
  waiting for transfers between devices  51.6 us (38%)
  starting transfers between devices  48.2 us (36%)
  Pallas kernels  17.9 us (13%)
  local copies, waits for them, and re-layouts  9.15 us (7%)
  other arithmetic  6.17 us (5%)
    ppermute x20, waiting for transfers between devices, xor_pass(): lax.ppermute(value, axis, [(i, i ^ bit) for i in range(lax.axis_size(axis...  29.5 us
    ppermute x12, starting transfers between devices, passed_along(): return lax.ppermute(value, axis, pairs)  25 us
    ppermute x20, starting transfers between devices, xor_pass(): lax.ppermute(value, axis, [(i, i ^ bit) for i in range(lax.axis_size(axis...  23.2 us
    ppermute x12, waiting for transfers between devices, passed_along(): return lax.ppermute(value, axis, pairs)  22.1 us
    pallas_call x1, Pallas kernels, body(): pl.pallas_call(backward_conv, out_shape=(jax.ShapeDtypeStruct((rows, PIX)...  8.57 us
    pallas_call x1, Pallas kernels, body(): pl.pallas_call(forward_conv, out_shape=(jax.ShapeDtypeStruct((rows, PIX),...  4.8 us
    pallas_call x1, Pallas kernels, body(): pl.pallas_call(mlp, out_shape=(jax.ShapeDtypeStruct((4, tile_count, chann...  4.5 us
  transfers between devices with their start and end apart: 32, of which 16 were waited for; matrix products, arithmetic and copies ran while one was open for 7% of the time, Pallas kernels for 10%

profile of v1, /device:TPU:0, one launch (start us, length us, event | category | flops | bytes accessed | tf_op | source)
XLA Modules:
  0.0 134.2 jit_solution(12946555439034370432)
XLA Ops:
  2.6 3.0 %collective-permute-start.1 = (s32[4]{0:T(128)S(1)}, s32[4]{0:T(128)S(1)}, u32[]{:S(2)}, u32[]{:S(2)}) collective-permute-start(s32[4]{0:T(128)S(1)} %broadcast_select_fusion), channel_id=1, source_target_pairs={{0,4},{4,0},{8,12},{12,8},{16,20},{20,16},{24,28},{28,24},{1,5},{5... | collective-permute-start | bytes 56 | tf_op jit(solution)/shard_map/ppermute | solution.py:204
  5.7 1.5 %gather_fusion = bf16[4,48,256]{2,1,0:T(8,128)(2,1)S(1)} fusion(bf16[16,48,256]{2,1,0:T(8,128)(2,1)} %param.12, s32[1024]{0:T(1024)S(1)} %pad_clamp_fusion.2), kind=kCustom, calls=%fused_computation | custom fusion | bytes 196624 | tf_op jit(solution)/shard_map/jit(_take)/gather | solution.py:237
  7.4 1.0 multiply_convert_fusion
  8.6 3.3 %collective-permute-done = bf16[4,48,256]{2,1,0:T(8,128)(2,1)S(1)} collective-permute-done((bf16[4,48,256]{2,1,0:T(8,128)(2,1)S(1)}, bf16[4,48,256]{2,1,0:T(8,128)(2,1)S(1)}, u32[]{:S(2)}, u32[]{:S(2)}) %collective-permute-start) | collective-permute-done | bytes 98336 | tf_op jit(solution)/shard_map/ppermute | solution.py:204
  11.9 1.0 pad_maximum_fusion
  13.5 3.4 %collective-permute-start.2 = (bf16[8,48,256]{2,1,0:T(8,128)(2,1)S(1)}, bf16[8,48,256]{2,1,0:T(8,128)(2,1)S(1)}, u32[]{:S(2)}, u32[]{:S(2)}) collective-permute-start(bf16[8,48,256]{2,1,0:T(8,128)(2,1)S(1)} %gather_fusion.1), channel_id=1, source_target_pairs={{0,12},{4,16},{8,20},{12,24},{16,28},{1,13},{5,17},{9,21},{13,25},... | collective-permute-start | bytes 589832 | tf_op jit(solution)/shard_map/ppermute | solution.py:210
  17.0 3.5 %collective-permute-start.3 = (bf16[8,48,256]{2,1,0:T(8,128)(2,1)S(1)}, bf16[8,48,256]{2,1,0:T(8,128)(2,1)S(1)}, u32[]{:S(2)}, u32[]{:S(2)}) collective-permute-start(bf16[8,48,256]{2,1,0:T(8,128)(2,1)S(1)} %gather_fusion.1), channel_id=1, source_target_pairs={{0,8},{4,12},{8,16},{12,20},{16,24},{20,28},{1,9},{5,13},{9,17},{1... | collective-permute-start | bytes 589832 | tf_op jit(solution)/shard_map/ppermute | solution.py:210
  21.1 4.4 %collective-permute-start.4 = (bf16[8,48,256]{2,1,0:T(8,128)(2,1)S(1)}, bf16[8,48,256]{2,1,0:T(8,128)(2,1)S(1)}, u32[]{:S(2)}, u32[]{:S(2)}) collective-permute-start(bf16[8,48,256]{2,1,0:T(8,128)(2,1)S(1)} %gather_fusion.1), channel_id=1, source_target_pairs={{0,4},{4,8},{8,12},{12,16},{16,20},{20,24},{24,28},{1,5},{5,9},{9,... | collective-permute-start | bytes 589832 | tf_op jit(solution)/shard_map/ppermute | solution.py:210
  25.6 1.3 collective-permute-start.5
  26.9 1.3 collective-permute-start.6
  28.9 1.3 collective-permute-start.7
  30.2 4.4 %collective-permute-done.4.p2 = bf16[8,48,256]{2,1,0:T(8,128)(2,1)S(1)} collective-permute-done((bf16[8,48,256]{2,1,0:T(8,128)(2,1)S(1)}, bf16[8,48,256]{2,1,0:T(8,128)(2,1)S(1)}, u32[]{:S(2)}, u32[]{:S(2)}) %collective-permute-start.4) | collective-permute-done | bytes 196640 | tf_op jit(solution)/shard_map/ppermute | solution.py:210
  34.6 1.5 %collective-permute-start.12 = (bf16[9,48,256]{2,1,0:T(8,128)(2,1)S(1)}, bf16[9,48,256]{2,1,0:T(8,128)(2,1)S(1)}, u32[]{:S(2)}, u32[]{:S(2)}) collective-permute-start(bf16[9,48,256]{2,1,0:T(8,128)(2,1)S(1)} %pad_maximum_fusion.1.d0), channel_id=1, source_target_pairs={{0,2},{1,3},{2,0},{3,1},{4,6},{5,7},{6,4},{7,5},{8,10},{9,11},{10,... | collective-permute-start | bytes 663560 | tf_op jit(solution)/shard_map/ppermute | solution.py:204
  36.1 2.9 %collective-permute-done.6.p5 = bf16[8,48,256]{2,1,0:T(8,128)(2,1)S(1)} collective-permute-done((bf16[8,48,256]{2,1,0:T(8,128)(2,1)S(1)}, bf16[8,48,256]{2,1,0:T(8,128)(2,1)S(1)}, u32[]{:S(2)}, u32[]{:S(2)}) %collective-permute-start.6) | collective-permute-done | bytes 196640 | tf_op jit(solution)/shard_map/ppermute | solution.py:210
  38.9 2.9 %collective-permute-done.7.p6 = bf16[8,48,256]{2,1,0:T(8,128)(2,1)S(1)} collective-permute-done((bf16[8,48,256]{2,1,0:T(8,128)(2,1)S(1)}, bf16[8,48,256]{2,1,0:T(8,128)(2,1)S(1)}, u32[]{:S(2)}, u32[]{:S(2)}) %collective-permute-start.7) | collective-permute-done | bytes 196640 | tf_op jit(solution)/shard_map/ppermute | solution.py:210
  41.8 0.9 copy-done.5
  42.7 4.8 %forward_conv.1 = (bf16[384,256]{1,0:T(8,128)(2,1)S(1)}, bf16[544,384]{1,0:T(8,128)(2,1)S(1)}) custom-call(s32[8,8]{1,0:T(8,128)S(1)} %and_select_fusion.ids, bf16[8,48,256]{2,1,0:T(8,128)(2,1)S(1)} %collective-permute-done.2.p0, bf16[8,48,256]{2,1,0:T(8,128)(2,1)S(1)} %copy-done.5, bf16[8,48,256]{2,1,0:T(8,128)(2,1)S(1)} %collective-permute-done.4.p2, ...), custom_call_target="tpu_custom_call" | custom-call | tf_op jit(solution)/shard_map/forward_conv/pallas_call | solution.py:283
  47.8 1.5 %collective-permute-start.8 = (bf16[8,48,256]{2,1,0:T(8,128)(2,1)S(1)}, bf16[8,48,256]{2,1,0:T(8,128)(2,1)}, u32[]{:S(2)}, u32[]{:S(2)}) collective-permute-start(bf16[8,48,256]{2,1,0:T(8,128)(2,1)S(1)} %bitcast.57), channel_id=1, source_target_pairs={{0,1},{1,0},{2,3},{3,2},{4,5},{5,4},{6,7},{7,6},{8,9},{9,8},{10,11... | collective-permute-start | bytes 589832 | tf_op jit(solution)/shard_map/ppermute | solution.py:204
  51.3 0.7 tile.20
  52.0 1.0 tile.21.weights
  53.1 1.7 %collective-permute-done.10.m3 = bf16[8,48,256]{2,1,0:T(8,128)(2,1)} collective-permute-done((bf16[8,48,256]{2,1,0:T(8,128)(2,1)S(1)}, bf16[8,48,256]{2,1,0:T(8,128)(2,1)}, u32[]{:S(2)}, u32[]{:S(2)}) %collective-permute-start.10) | collective-permute-done | bytes 196640 | tf_op jit(solution)/shard_map/ppermute | solution.py:204
  54.9 4.3 %collective-permute-done.9.m2 = bf16[8,48,256]{2,1,0:T(8,128)(2,1)} collective-permute-done((bf16[8,48,256]{2,1,0:T(8,128)(2,1)S(1)}, bf16[8,48,256]{2,1,0:T(8,128)(2,1)}, u32[]{:S(2)}, u32[]{:S(2)}) %collective-permute-start.9) | collective-permute-done | bytes 196640 | tf_op jit(solution)/shard_map/ppermute | solution.py:204
  59.1 4.5 %mlp.1 = (bf16[4,8,48,256]{3,2,1,0:T(8,128)(2,1)S(1)}, bf16[4,9,48,256]{3,2,1,0:T(8,128)(2,1)S(1)}, bf16[8,48,192]{2,1,0:T(8,128)(2,1)S(1)}, f32[2,8,256]{2,1,0:T(8,128)S(1)}) custom-call(s32[4]{0:T(128)S(1)} %iota_xor_fusion.perm, bf16[8,48,256]{2,1,0:T(8,128)(2,1)S(1)} %bitcast.59, bf16[8,48,256]{2,1,0:T(8,128)(2,1)} %collective-permute-done.8.m1, ...), custom_call_target="tpu_custom_call" | custom-call | tf_op jit(solution)/shard_map/mlp/pallas_call | solution.py:299
  63.6 6.3 %collective-permute-start.29 = (bf16[8,48,192]{2,1,0:T(8,128)(2,1)S(1)}, bf16[8,48,192]{2,1,0:T(8,128)(2,1)S(1)}, u32[]{:S(2)}, u32[]{:S(2)}) collective-permute-start(bf16[8,48,192]{2,1,0:T(8,128)(2,1)S(1)} %get-tuple-element.20), channel_id=1, source_target_pairs={{0,4},{4,0},{8,12},{12,8},{16,20},{20,16},{24,28},{28,24},{1,5},{5... | collective-permute-start | bytes 442376 | tf_op jit(solution)/shard_map/ppermute | solution.py:204
  70.0 1.1 collective-permute-start.18
  71.1 0.8 collective-permute-start.19
  71.9 6.4 %collective-permute-done.18 = bf16[9,48,256]{2,1,0:T(8,128)(2,1)S(1)} collective-permute-done((bf16[9,48,256]{2,1,0:T(8,128)(2,1)S(1)}, bf16[9,48,256]{2,1,0:T(8,128)(2,1)S(1)}, u32[]{:S(2)}, u32[]{:S(2)}) %collective-permute-start.18) | collective-permute-done | bytes 221216 | tf_op jit(solution)/shard_map/ppermute | solution.py:204
  78.3 3.8 %collective-permute-done.19 = bf16[9,48,256]{2,1,0:T(8,128)(2,1)S(1)} collective-permute-done((bf16[9,48,256]{2,1,0:T(8,128)(2,1)S(1)}, bf16[9,48,256]{2,1,0:T(8,128)(2,1)S(1)}, u32[]{:S(2)}, u32[]{:S(2)}) %collective-permute-start.19) | collective-permute-done | bytes 221216 | tf_op jit(solution)/shard_map/ppermute | solution.py:204
  82.4 1.4 %collective-permute-start.20 = (bf16[8,48,256]{2,1,0:T(8,128)(2,1)S(1)}, bf16[8,48,256]{2,1,0:T(8,128)(2,1)S(1)}, u32[]{:S(2)}, u32[]{:S(2)}) collective-permute-start(bf16[8,48,256]{2,1,0:T(8,128)(2,1)S(1)} %fusion.3.p3), channel_id=1, source_target_pairs={{0,12},{4,16},{8,20},{12,24},{16,28},{1,13},{5,17},{9,21},{13,25},... | collective-permute-start | bytes 589832 | tf_op jit(solution)/shard_map/ppermute | solution.py:210
  83.9 2.6 %collective-permute-start.21 = (bf16[8,48,256]{2,1,0:T(8,128)(2,1)S(1)}, bf16[8,48,256]{2,1,0:T(8,128)(2,1)S(1)}, u32[]{:S(2)}, u32[]{:S(2)}) collective-permute-start(bf16[8,48,256]{2,1,0:T(8,128)(2,1)S(1)} %fusion.3.p3), channel_id=1, source_target_pairs={{0,8},{4,12},{8,16},{12,20},{16,24},{20,28},{1,9},{5,13},{9,17},{1... | collective-permute-start | bytes 589832 | tf_op jit(solution)/shard_map/ppermute | solution.py:210
  86.7 1.8 %collective-permute-start.22 = (bf16[8,48,256]{2,1,0:T(8,128)(2,1)S(1)}, bf16[8,48,256]{2,1,0:T(8,128)(2,1)S(1)}, u32[]{:S(2)}, u32[]{:S(2)}) collective-permute-start(bf16[8,48,256]{2,1,0:T(8,128)(2,1)S(1)} %fusion.3.p3), channel_id=1, source_target_pairs={{0,4},{4,8},{8,12},{12,16},{16,20},{20,24},{24,28},{1,5},{5,9},{9,... | collective-permute-start | bytes 589832 | tf_op jit(solution)/shard_map/ppermute | solution.py:210
  88.5 1.3 collective-permute-start.23
  89.8 1.3 collective-permute-start.24
  91.1 2.2 %collective-permute-done.21.p1 = bf16[8,48,256]{2,1,0:T(8,128)(2,1)S(1)} collective-permute-done((bf16[8,48,256]{2,1,0:T(8,128)(2,1)S(1)}, bf16[8,48,256]{2,1,0:T(8,128)(2,1)S(1)}, u32[]{:S(2)}, u32[]{:S(2)}) %collective-permute-start.21) | collective-permute-done | bytes 196640 | tf_op jit(solution)/shard_map/ppermute | solution.py:210
  93.3 1.3 collective-permute-start.25
  94.7 3.5 %collective-permute-done.23.p4 = bf16[8,48,256]{2,1,0:T(8,128)(2,1)S(1)} collective-permute-done((bf16[8,48,256]{2,1,0:T(8,128)(2,1)S(1)}, bf16[8,48,256]{2,1,0:T(8,128)(2,1)S(1)}, u32[]{:S(2)}, u32[]{:S(2)}) %collective-permute-start.23) | collective-permute-done | bytes 196640 | tf_op jit(solution)/shard_map/ppermute | solution.py:210
  98.2 1.0 collective-permute-start.15
  99.2 5.1 %collective-permute-done.24.p5 = bf16[8,48,256]{2,1,0:T(8,128)(2,1)S(1)} collective-permute-done((bf16[8,48,256]{2,1,0:T(8,128)(2,1)S(1)}, bf16[8,48,256]{2,1,0:T(8,128)(2,1)S(1)}, u32[]{:S(2)}, u32[]{:S(2)}) %collective-permute-start.24) | collective-permute-done | bytes 196640 | tf_op jit(solution)/shard_map/ppermute | solution.py:210
  104.3 1.2 collective-permute-done.25.p6
  105.5 8.6 %backward_conv.1 = (bf16[384,256]{1,0:T(8,128)(2,1)}, f32[56,48]{1,0:T(8,128)S(1)}) custom-call(s32[8,8]{1,0:T(8,128)S(1)} %and_select_fusion.ids, bf16[8,48,256]{2,1,0:T(8,128)(2,1)S(1)} %collective-permute-done.20.p0, bf16[8,48,256]{2,1,0:T(8,128)(2,1)S(1)} %collective-permute-done.21.p1, bf16[8,48,256]{2,1,0:T(8,128)(2,1)S(1)} %collective-permute-done.22.p2, ...), custom_call_target="tpu_custom_call" | custom-call | tf_op jit(solution)/shard_map/backward_conv/pallas_call | solution.py:345
  114.1 6.8 %collective-permute-start.26 = (f32[56,48]{1,0:T(8,128)S(1)}, f32[56,48]{1,0:T(8,128)S(1)}, u32[]{:S(2)}, u32[]{:S(2)}) collective-permute-start(f32[56,48]{1,0:T(8,128)S(1)} %get-tuple-element.19), channel_id=1, source_target_pairs={{0,4},{4,0},{8,12},{12,8},{16,20},{20,16},{24,28},{28,24},{1,5},{5... | collective-permute-start | bytes 32264 | tf_op jit(solution)/shard_map/ppermute | solution.py:204
  121.1 1.7 %collective-permute-done.26 = f32[56,48]{1,0:T(8,128)S(1)} collective-permute-done((f32[56,48]{1,0:T(8,128)S(1)}, f32[56,48]{1,0:T(8,128)S(1)}, u32[]{:S(2)}, u32[]{:S(2)}) %collective-permute-start.26) | collective-permute-done | bytes 10784 | tf_op jit(solution)/shard_map/ppermute | solution.py:204
  122.8 0.8 add_convert_fusion
  123.7 5.1 %collective-permute-done.27 = f32[56,48]{1,0:T(8,128)S(1)} collective-permute-done((f32[56,48]{1,0:T(8,128)S(1)}, f32[56,48]{1,0:T(8,128)S(1)}, u32[]{:S(2)}, u32[]{:S(2)}) %collective-permute-start.27) | collective-permute-done | bytes 10784 | tf_op jit(solution)/shard_map/ppermute | solution.py:204
  128.7 2.1 %collective-permute-done.31 = bf16[8,48,192]{2,1,0:T(8,128)(2,1)S(1)} collective-permute-done((bf16[8,48,192]{2,1,0:T(8,128)(2,1)S(1)}, bf16[8,48,192]{2,1,0:T(8,128)(2,1)S(1)}, u32[]{:S(2)}, u32[]{:S(2)}) %collective-permute-start.31) | collective-permute-done | bytes 147488 | tf_op jit(solution)/shard_map/ppermute | solution.py:204
  130.9 0.7 slice_multiply_fusion.1
  131.6 0.8 copy.40
  132.4 1.1 collective-permute-done.28
  (100 shorter events, 7.9 us)
Async XLA Ops:
  0.6 49.8 %copy-start = (bf16[192,192]{1,0:T(8,128)(2,1)S(1)}, bf16[192,192]{1,0:T(8,128)(2,1)}, u32[]{:S(2)}) copy-start(bf16[192,192]{1,0:T(8,128)(2,1)} %param.18) | copy-start | bytes 221188
  0.6 19.8 %copy-start.10 = (bf16[48]{0:T(256)(128)(2,1)S(1)}, bf16[48]{0:T(256)(128)(2,1)}, u32[]{:S(2)}) copy-start(bf16[48]{0:T(256)(128)(2,1)} %param.17) | copy-start | bytes 292
  2.6 5.9 %collective-permute-start.1 = (s32[4]{0:T(128)S(1)}, s32[4]{0:T(128)S(1)}, u32[]{:S(2)}, u32[]{:S(2)}) collective-permute-start(s32[4]{0:T(128)S(1)} %broadcast_select_fusion), channel_id=1, source_target_pairs={{0,4},{4,0},{8,12},{12,8},{16,20},{20,16},{24,28},{28,24},{1,5},{5... | collective-permute-start | bytes 56 | tf_op jit(solution)/shard_map/ppermute | solution.py:204
  7.2 4.7 %collective-permute-start = (bf16[4,48,256]{2,1,0:T(8,128)(2,1)S(1)}, bf16[4,48,256]{2,1,0:T(8,128)(2,1)S(1)}, u32[]{:S(2)}, u32[]{:S(2)}) collective-permute-start(bf16[4,48,256]{2,1,0:T(8,128)(2,1)S(1)} %gather_fusion), channel_id=1, source_target_pairs={{0,4},{4,0},{8,12},{12,8},{16,20},{20,16},{24,28},{28,24},{1,5},{5... | collective-permute-start | bytes 294920 | tf_op jit(solution)/shard_map/ppermute | solution.py:204
  7.4 13.2 %copy-start.7 = (f32[48,49]{1,0:T(8,128)S(1)}, f32[48,49]{1,0:T(8,128)}, u32[]{:S(2)}) copy-start(f32[48,49]{1,0:T(8,128)} %param.16) | copy-start | bytes 28228
  8.6 12.4 %copy-start.6 = (bf16[192,192]{1,0:T(8,128)(2,1)S(1)}, bf16[192,192]{1,0:T(8,128)(2,1)}, u32[]{:S(2)}) copy-start(bf16[192,192]{1,0:T(8,128)(2,1)} %param.20) | copy-start | bytes 221188
  8.6 21.6 %copy-start.8 = (s32[8,8]{1,0:T(8,128)S(1)}, s32[8,8]{1,0:T(8,128)}, u32[]{:S(2)}) copy-start(s32[8,8]{1,0:T(8,128)} %param.14) | copy-start | bytes 772
  8.6 33.2 %copy-start.1 = (bf16[544,1024]{1,0:T(8,128)(2,1)S(1)}, bf16[544,1024]{1,0:T(8,128)(2,1)}, u32[]{:S(2)}) copy-start(bf16[544,1024]{1,0:T(8,128)(2,1)} %constant.68.clone.place) | copy-start | bytes 3342340
  13.5 13.4 %collective-permute-start.2 = (bf16[8,48,256]{2,1,0:T(8,128)(2,1)S(1)}, bf16[8,48,256]{2,1,0:T(8,128)(2,1)S(1)}, u32[]{:S(2)}, u32[]{:S(2)}) collective-permute-start(bf16[8,48,256]{2,1,0:T(8,128)(2,1)S(1)} %gather_fusion.1), channel_id=1, source_target_pairs={{0,12},{4,16},{8,20},{12,24},{16,28},{1,13},{5,17},{9,21},{13,25},... | collective-permute-start | bytes 589832 | tf_op jit(solution)/shard_map/ppermute | solution.py:210
  17.0 11.2 %collective-permute-start.3 = (bf16[8,48,256]{2,1,0:T(8,128)(2,1)S(1)}, bf16[8,48,256]{2,1,0:T(8,128)(2,1)S(1)}, u32[]{:S(2)}, u32[]{:S(2)}) collective-permute-start(bf16[8,48,256]{2,1,0:T(8,128)(2,1)S(1)} %gather_fusion.1), channel_id=1, source_target_pairs={{0,8},{4,12},{8,16},{12,20},{16,24},{20,28},{1,9},{5,13},{9,17},{1... | collective-permute-start | bytes 589832 | tf_op jit(solution)/shard_map/ppermute | solution.py:210
  20.6 28.6 %collective-permute-start.11 = (bf16[9,48,256]{2,1,0:T(8,128)(2,1)S(1)}, bf16[9,48,256]{2,1,0:T(8,128)(2,1)S(1)}, u32[]{:S(2)}, u32[]{:S(2)}) collective-permute-start(bf16[9,48,256]{2,1,0:T(8,128)(2,1)S(1)} %pad_maximum_fusion.1.d0), channel_id=1, source_target_pairs={{0,1},{1,0},{2,3},{3,2},{4,5},{5,4},{6,7},{7,6},{8,9},{9,8},{10,11... | collective-permute-start | bytes 663560 | tf_op jit(solution)/shard_map/ppermute | solution.py:204
  21.1 13.5 %collective-permute-start.4 = (bf16[8,48,256]{2,1,0:T(8,128)(2,1)S(1)}, bf16[8,48,256]{2,1,0:T(8,128)(2,1)S(1)}, u32[]{:S(2)}, u32[]{:S(2)}) collective-permute-start(bf16[8,48,256]{2,1,0:T(8,128)(2,1)S(1)} %gather_fusion.1), channel_id=1, source_target_pairs={{0,4},{4,8},{8,12},{12,16},{16,20},{20,24},{24,28},{1,5},{5,9},{9,... | collective-permute-start | bytes 589832 | tf_op jit(solution)/shard_map/ppermute | solution.py:210
  25.6 10.5 %collective-permute-start.5 = (bf16[8,48,256]{2,1,0:T(8,128)(2,1)S(1)}, bf16[8,48,256]{2,1,0:T(8,128)(2,1)S(1)}, u32[]{:S(2)}, u32[]{:S(2)}) collective-permute-start(bf16[8,48,256]{2,1,0:T(8,128)(2,1)S(1)} %gather_fusion.1), channel_id=1, source_target_pairs={{4,0},{8,4},{12,8},{16,12},{20,16},{24,20},{28,24},{5,1},{9,5},{13... | collective-permute-start | bytes 589832 | tf_op jit(solution)/shard_map/ppermute | solution.py:210
  26.9 12.1 %collective-permute-start.6 = (bf16[8,48,256]{2,1,0:T(8,128)(2,1)S(1)}, bf16[8,48,256]{2,1,0:T(8,128)(2,1)S(1)}, u32[]{:S(2)}, u32[]{:S(2)}) collective-permute-start(bf16[8,48,256]{2,1,0:T(8,128)(2,1)S(1)} %gather_fusion.1), channel_id=1, source_target_pairs={{8,0},{12,4},{16,8},{20,12},{24,16},{28,20},{9,1},{13,5},{17,9},{2... | collective-permute-start | bytes 589832 | tf_op jit(solution)/shard_map/ppermute | solution.py:210
  28.2 0.7 copy-start.4
  28.9 12.9 %collective-permute-start.7 = (bf16[8,48,256]{2,1,0:T(8,128)(2,1)S(1)}, bf16[8,48,256]{2,1,0:T(8,128)(2,1)S(1)}, u32[]{:S(2)}, u32[]{:S(2)}) collective-permute-start(bf16[8,48,256]{2,1,0:T(8,128)(2,1)S(1)} %gather_fusion.1), channel_id=1, source_target_pairs={{12,0},{16,4},{20,8},{24,12},{28,16},{13,1},{17,5},{21,9},{25,13},... | collective-permute-start | bytes 589832 | tf_op jit(solution)/shard_map/ppermute | solution.py:210
  30.2 20.9 %copy-start.11 = (bf16[192]{0:T(256)(128)(2,1)S(1)}, bf16[192]{0:T(256)(128)(2,1)}, u32[]{:S(2)}) copy-start(bf16[192]{0:T(256)(128)(2,1)} %param.19) | copy-start | bytes 1156
  34.6 18.5 %collective-permute-start.12 = (bf16[9,48,256]{2,1,0:T(8,128)(2,1)S(1)}, bf16[9,48,256]{2,1,0:T(8,128)(2,1)S(1)}, u32[]{:S(2)}, u32[]{:S(2)}) collective-permute-start(bf16[9,48,256]{2,1,0:T(8,128)(2,1)S(1)} %pad_maximum_fusion.1.d0), channel_id=1, source_target_pairs={{0,2},{1,3},{2,0},{3,1},{4,6},{5,7},{6,4},{7,5},{8,10},{9,11},{10,... | collective-permute-start | bytes 663560 | tf_op jit(solution)/shard_map/ppermute | solution.py:204
  36.1 17.0 %collective-permute-start.13 = (bf16[9,48,256]{2,1,0:T(8,128)(2,1)S(1)}, bf16[9,48,256]{2,1,0:T(8,128)(2,1)S(1)}, u32[]{:S(2)}, u32[]{:S(2)}) collective-permute-start(bf16[9,48,256]{2,1,0:T(8,128)(2,1)S(1)} %pad_maximum_fusion.1.d0), channel_id=1, source_target_pairs={{0,3},{1,2},{2,1},{3,0},{4,7},{5,6},{6,5},{7,4},{8,11},{9,10},{10,... | collective-permute-start | bytes 663560 | tf_op jit(solution)/shard_map/ppermute | solution.py:204
  41.8 0.9 copy-start.5
  47.5 7.3 %collective-permute-start.10 = (bf16[8,48,256]{2,1,0:T(8,128)(2,1)S(1)}, bf16[8,48,256]{2,1,0:T(8,128)(2,1)}, u32[]{:S(2)}, u32[]{:S(2)}) collective-permute-start(bf16[8,48,256]{2,1,0:T(8,128)(2,1)S(1)} %bitcast.56), channel_id=1, source_target_pairs={{0,3},{1,2},{2,1},{3,0},{4,7},{5,6},{6,5},{7,4},{8,11},{9,10},{10,... | collective-permute-start | bytes 589832 | tf_op jit(solution)/shard_map/ppermute | solution.py:204
  47.8 7.1 %collective-permute-start.8 = (bf16[8,48,256]{2,1,0:T(8,128)(2,1)S(1)}, bf16[8,48,256]{2,1,0:T(8,128)(2,1)}, u32[]{:S(2)}, u32[]{:S(2)}) collective-permute-start(bf16[8,48,256]{2,1,0:T(8,128)(2,1)S(1)} %bitcast.57), channel_id=1, source_target_pairs={{0,1},{1,0},{2,3},{3,2},{4,5},{5,4},{6,7},{7,6},{8,9},{9,8},{10,11... | collective-permute-start | bytes 589832 | tf_op jit(solution)/shard_map/ppermute | solution.py:204
  49.2 9.9 %collective-permute-start.9 = (bf16[8,48,256]{2,1,0:T(8,128)(2,1)S(1)}, bf16[8,48,256]{2,1,0:T(8,128)(2,1)}, u32[]{:S(2)}, u32[]{:S(2)}) collective-permute-start(bf16[8,48,256]{2,1,0:T(8,128)(2,1)S(1)} %bitcast.58), channel_id=1, source_target_pairs={{0,2},{1,3},{2,0},{3,1},{4,6},{5,7},{6,4},{7,5},{8,10},{9,11},{10,... | collective-permute-start | bytes 589832 | tf_op jit(solution)/shard_map/ppermute | solution.py:204
  63.6 22.9 %collective-permute-start.29 = (bf16[8,48,192]{2,1,0:T(8,128)(2,1)S(1)}, bf16[8,48,192]{2,1,0:T(8,128)(2,1)S(1)}, u32[]{:S(2)}, u32[]{:S(2)}) collective-permute-start(bf16[8,48,192]{2,1,0:T(8,128)(2,1)S(1)} %get-tuple-element.20), channel_id=1, source_target_pairs={{0,4},{4,0},{8,12},{12,8},{16,20},{20,16},{24,28},{28,24},{1,5},{5... | collective-permute-start | bytes 442376 | tf_op jit(solution)/shard_map/ppermute | solution.py:204
  69.9 1.9 %collective-permute-start.17 = (bf16[9,48,256]{2,1,0:T(8,128)(2,1)S(1)}, bf16[9,48,256]{2,1,0:T(8,128)(2,1)S(1)}, u32[]{:S(2)}, u32[]{:S(2)}) collective-permute-start(bf16[9,48,256]{2,1,0:T(8,128)(2,1)S(1)} %get-tuple-element.44), channel_id=1, source_target_pairs={{0,1},{1,0},{2,3},{3,2},{4,5},{5,4},{6,7},{7,6},{8,9},{9,8},{10,11... | collective-permute-start | bytes 663560 | tf_op jit(solution)/shard_map/ppermute | solution.py:204
  70.0 8.3 %collective-permute-start.18 = (bf16[9,48,256]{2,1,0:T(8,128)(2,1)S(1)}, bf16[9,48,256]{2,1,0:T(8,128)(2,1)S(1)}, u32[]{:S(2)}, u32[]{:S(2)}) collective-permute-start(bf16[9,48,256]{2,1,0:T(8,128)(2,1)S(1)} %get-tuple-element.46), channel_id=1, source_target_pairs={{0,2},{1,3},{2,0},{3,1},{4,6},{5,7},{6,4},{7,5},{8,10},{9,11},{10,... | collective-permute-start | bytes 663560 | tf_op jit(solution)/shard_map/ppermute | solution.py:204
  71.1 11.0 %collective-permute-start.19 = (bf16[9,48,256]{2,1,0:T(8,128)(2,1)S(1)}, bf16[9,48,256]{2,1,0:T(8,128)(2,1)S(1)}, u32[]{:S(2)}, u32[]{:S(2)}) collective-permute-start(bf16[9,48,256]{2,1,0:T(8,128)(2,1)S(1)} %get-tuple-element.45), channel_id=1, source_target_pairs={{0,3},{1,2},{2,1},{3,0},{4,7},{5,6},{6,5},{7,4},{8,11},{9,10},{10,... | collective-permute-start | bytes 663560 | tf_op jit(solution)/shard_map/ppermute | solution.py:204
  82.3 23.2 %copy-start.2 = (bf16[8,48,256]{2,1,0:T(8,128)(2,1)S(1)}, bf16[8,48,256]{2,1,0:T(8,128)(2,1)}, u32[]{:S(2)}) copy-start(bf16[8,48,256]{2,1,0:T(8,128)(2,1)} %param.15) | copy-start | bytes 589828
  82.3 23.2 %copy-start.3 = (f32[384,48]{1,0:T(8,128)S(1)}, f32[384,48]{1,0:T(8,128)}, u32[]{:S(2)}) copy-start(f32[384,48]{1,0:T(8,128)} %constant.69.clone.fold) | copy-start | bytes 221188
  82.4 7.4 %collective-permute-start.20 = (bf16[8,48,256]{2,1,0:T(8,128)(2,1)S(1)}, bf16[8,48,256]{2,1,0:T(8,128)(2,1)S(1)}, u32[]{:S(2)}, u32[]{:S(2)}) collective-permute-start(bf16[8,48,256]{2,1,0:T(8,128)(2,1)S(1)} %fusion.3.p3), channel_id=1, source_target_pairs={{0,12},{4,16},{8,20},{12,24},{16,28},{1,13},{5,17},{9,21},{13,25},... | collective-permute-start | bytes 589832 | tf_op jit(solution)/shard_map/ppermute | solution.py:210
  83.9 9.4 %collective-permute-start.21 = (bf16[8,48,256]{2,1,0:T(8,128)(2,1)S(1)}, bf16[8,48,256]{2,1,0:T(8,128)(2,1)S(1)}, u32[]{:S(2)}, u32[]{:S(2)}) collective-permute-start(bf16[8,48,256]{2,1,0:T(8,128)(2,1)S(1)} %fusion.3.p3), channel_id=1, source_target_pairs={{0,8},{4,12},{8,16},{12,20},{16,24},{20,28},{1,9},{5,13},{9,17},{1... | collective-permute-start | bytes 589832 | tf_op jit(solution)/shard_map/ppermute | solution.py:210
  86.6 34.3 %collective-permute-start.30 = (bf16[8,48,192]{2,1,0:T(8,128)(2,1)S(1)}, bf16[8,48,192]{2,1,0:T(8,128)(2,1)S(1)}, u32[]{:S(2)}, u32[]{:S(2)}) collective-permute-start(bf16[8,48,192]{2,1,0:T(8,128)(2,1)S(1)} %reduce-precision_convert_fusion.1), channel_id=1, source_target_pairs={{0,8},{4,12},{8,0},{12,4},{16,24},{20,28},{24,16},{28,20},{1,9},{5... | collective-permute-start | bytes 442376 | tf_op jit(solution)/shard_map/ppermute | solution.py:204
  86.7 7.9 %collective-permute-start.22 = (bf16[8,48,256]{2,1,0:T(8,128)(2,1)S(1)}, bf16[8,48,256]{2,1,0:T(8,128)(2,1)S(1)}, u32[]{:S(2)}, u32[]{:S(2)}) collective-permute-start(bf16[8,48,256]{2,1,0:T(8,128)(2,1)S(1)} %fusion.3.p3), channel_id=1, source_target_pairs={{0,4},{4,8},{8,12},{12,16},{16,20},{20,24},{24,28},{1,5},{5,9},{9,... | collective-permute-start | bytes 589832 | tf_op jit(solution)/shard_map/ppermute | solution.py:210
  88.5 9.7 %collective-permute-start.23 = (bf16[8,48,256]{2,1,0:T(8,128)(2,1)S(1)}, bf16[8,48,256]{2,1,0:T(8,128)(2,1)S(1)}, u32[]{:S(2)}, u32[]{:S(2)}) collective-permute-start(bf16[8,48,256]{2,1,0:T(8,128)(2,1)S(1)} %fusion.3.p3), channel_id=1, source_target_pairs={{4,0},{8,4},{12,8},{16,12},{20,16},{24,20},{28,24},{5,1},{9,5},{13... | collective-permute-start | bytes 589832 | tf_op jit(solution)/shard_map/ppermute | solution.py:210
  89.8 14.5 %collective-permute-start.24 = (bf16[8,48,256]{2,1,0:T(8,128)(2,1)S(1)}, bf16[8,48,256]{2,1,0:T(8,128)(2,1)S(1)}, u32[]{:S(2)}, u32[]{:S(2)}) collective-permute-start(bf16[8,48,256]{2,1,0:T(8,128)(2,1)S(1)} %fusion.3.p3), channel_id=1, source_target_pairs={{8,0},{12,4},{16,8},{20,12},{24,16},{28,20},{9,1},{13,5},{17,9},{2... | collective-permute-start | bytes 589832 | tf_op jit(solution)/shard_map/ppermute | solution.py:210
  93.3 12.2 %collective-permute-start.25 = (bf16[8,48,256]{2,1,0:T(8,128)(2,1)S(1)}, bf16[8,48,256]{2,1,0:T(8,128)(2,1)S(1)}, u32[]{:S(2)}, u32[]{:S(2)}) collective-permute-start(bf16[8,48,256]{2,1,0:T(8,128)(2,1)S(1)} %fusion.3.p3), channel_id=1, source_target_pairs={{12,0},{16,4},{20,8},{24,12},{28,16},{13,1},{17,5},{21,9},{25,13},... | collective-permute-start | bytes 589832 | tf_op jit(solution)/shard_map/ppermute | solution.py:210
  94.6 28.2 %collective-permute-start.14 = (bf16[8,48,256]{2,1,0:T(8,128)(2,1)S(1)}, bf16[8,48,256]{2,1,0:T(8,128)(2,1)S(1)}, u32[]{:S(2)}, u32[]{:S(2)}) collective-permute-start(bf16[8,48,256]{2,1,0:T(8,128)(2,1)S(1)} %get-tuple-element.47), channel_id=1, source_target_pairs={{0,1},{1,0},{2,3},{3,2},{4,5},{5,4},{6,7},{7,6},{8,9},{9,8},{10,11... | collective-permute-start | bytes 589832 | tf_op jit(solution)/shard_map/ppermute | solution.py:204
  98.2 24.6 %collective-permute-start.15 = (bf16[8,48,256]{2,1,0:T(8,128)(2,1)S(1)}, bf16[8,48,256]{2,1,0:T(8,128)(2,1)S(1)}, u32[]{:S(2)}, u32[]{:S(2)}) collective-permute-start(bf16[8,48,256]{2,1,0:T(8,128)(2,1)S(1)} %get-tuple-element.49), channel_id=1, source_target_pairs={{0,2},{1,3},{2,0},{3,1},{4,6},{5,7},{6,4},{7,5},{8,10},{9,11},{10,... | collective-permute-start | bytes 589832 | tf_op jit(solution)/shard_map/ppermute | solution.py:204
  104.3 18.5 %collective-permute-start.16 = (bf16[8,48,256]{2,1,0:T(8,128)(2,1)S(1)}, bf16[8,48,256]{2,1,0:T(8,128)(2,1)S(1)}, u32[]{:S(2)}, u32[]{:S(2)}) collective-permute-start(bf16[8,48,256]{2,1,0:T(8,128)(2,1)S(1)} %get-tuple-element.48), channel_id=1, source_target_pairs={{0,3},{1,2},{2,1},{3,0},{4,7},{5,6},{6,5},{7,4},{8,11},{9,10},{10,... | collective-permute-start | bytes 589832 | tf_op jit(solution)/shard_map/ppermute | solution.py:204
  105.5 17.3 %copy-start.9 = (f32[48]{0:T(128)S(1)}, f32[48]{0:T(128)}, u32[]{:S(2)}) copy-start(f32[48]{0:T(128)} %param.21) | copy-start | bytes 580
  114.1 8.7 %collective-permute-start.26 = (f32[56,48]{1,0:T(8,128)S(1)}, f32[56,48]{1,0:T(8,128)S(1)}, u32[]{:S(2)}, u32[]{:S(2)}) collective-permute-start(f32[56,48]{1,0:T(8,128)S(1)} %get-tuple-element.19), channel_id=1, source_target_pairs={{0,4},{4,0},{8,12},{12,8},{16,20},{20,16},{24,28},{28,24},{1,5},{5... | collective-permute-start | bytes 32264 | tf_op jit(solution)/shard_map/ppermute | solution.py:204
  121.0 9.9 %collective-permute-start.31 = (bf16[8,48,192]{2,1,0:T(8,128)(2,1)S(1)}, bf16[8,48,192]{2,1,0:T(8,128)(2,1)S(1)}, u32[]{:S(2)}, u32[]{:S(2)}) collective-permute-start(bf16[8,48,192]{2,1,0:T(8,128)(2,1)S(1)} %reduce-precision_convert_fusion), channel_id=1, source_target_pairs={{0,16},{4,20},{8,24},{12,28},{16,0},{20,4},{24,8},{28,12},{1,17},{... | collective-permute-start | bytes 442376 | tf_op jit(solution)/shard_map/ppermute | solution.py:204
  122.8 5.9 %collective-permute-start.27 = (f32[56,48]{1,0:T(8,128)S(1)}, f32[56,48]{1,0:T(8,128)S(1)}, u32[]{:S(2)}, u32[]{:S(2)}) collective-permute-start(f32[56,48]{1,0:T(8,128)S(1)} %add.99), channel_id=1, source_target_pairs={{0,8},{4,12},{8,0},{12,4},{16,24},{20,28},{24,16},{28,20},{1,9},{5... | collective-permute-start | bytes 32264 | tf_op jit(solution)/shard_map/ppermute | solution.py:204
  128.7 4.8 %collective-permute-start.28 = (f32[56,48]{1,0:T(8,128)S(1)}, f32[56,48]{1,0:T(8,128)S(1)}, u32[]{:S(2)}, u32[]{:S(2)}) collective-permute-start(f32[56,48]{1,0:T(8,128)S(1)} %add.100), channel_id=1, source_target_pairs={{0,16},{4,20},{8,24},{12,28},{16,0},{20,4},{24,8},{28,12},{1,17},{... | collective-permute-start | bytes 32264 | tf_op jit(solution)/shard_map/ppermute | solution.py:204

commit v2 on v1

--- a/solution.py
+++ b/solution.py
@@ -1,3 +1,4 @@
+import functools
 import math
 
 import jax
@@ -84,14 +85,61 @@
 
 
 def load_table(pieces, table):
-    for o in range(7):
-        table[o * 8 : o * 8 + 8] = pieces[o][...]
+    table[0:56] = pieces[...]
     table[56] = jnp.zeros((48, PIX), BF16)
 
 
-def forward_conv(ids, p0, p1, p2, p3, p4, p5, p6, place, weights, mixed, padded,
+def exchange(length, own, table, local_sem, send_sems, recv_sems):
+    me = lax.axis_index("tiles")
+    barrier = pltpu.get_barrier_semaphore()
+    offsets = [d for d in (3, -3, 2, -2, 1, -1) if abs(d) < length]
+
+    def each(action):
+        for d in offsets:
+            inside = (me + d >= 0) & (me + d < length)
+            pl.when(inside)(lambda d=d: action(d))
+
+    def greet(d):
+        pl.semaphore_signal(
+            barrier, inc=1, device_id={"tiles": me + d}, device_id_type=pl.DeviceIdType.MESH
+        )
+
+    def copy(d):
+        slot = REACH - d
+        return pltpu.make_async_remote_copy(
+            src_ref=own,
+            dst_ref=table.at[pl.ds(slot * 8, 8)],
+            send_sem=send_sems.at[slot],
+            recv_sem=recv_sems.at[slot],
+            device_id={"tiles": me + d},
+            device_id_type=pl.DeviceIdType.MESH,
+        )
+
+    def arrival(d):
+        slot = REACH + d
+        return pltpu.make_async_remote_copy(
+            src_ref=own,
+            dst_ref=table.at[pl.ds(slot * 8, 8)],
+            send_sem=send_sems.at[slot],
+            recv_sem=recv_sems.at[slot],
+            device_id={"tiles": me + d},
+            device_id_type=pl.DeviceIdType.MESH,
+        )
+
+    each(greet)
+    mine = pltpu.make_async_copy(own, table.at[pl.ds(REACH * 8, 8)], local_sem)
+    mine.start()
+    peers = jnp.minimum(me, REACH) + jnp.minimum(length - 1 - me, REACH)
+    pl.semaphore_wait(barrier, peers)
+    each(lambda d: copy(d).start())
+    mine.wait()
+    each(lambda d: copy(d).wait_send())
+    each(lambda d: arrival(d).wait_recv())
+
+
+def forward_conv(ids, pieces, place, weights, mixed, padded,
                  table, joined, pad, shifted, result):
-    load_table((p0, p1, p2, p3, p4, p5, p6), table)
+    load_table(pieces, table)
     fill_padded(ids, table, place, joined, pad)
     padded[...] = pad[...].astype(BF16)
     shift_copies(pad, shifted)
@@ -99,20 +147,17 @@
     mixed[...] = result[...].T.astype(BF16)
 
 
-def backward_conv(ids, p0, p1, p2, p3, p4, p5, p6, place, weights, padded, cotangent, fold,
-                  grad_in, grad_dw, table, joined, pad, shifted, result, taps):
-    load_table((p0, p1, p2, p3, p4, p5, p6), table)
+def backward_conv(ids, pieces, place, weights, cotangent,
+                  grad_in, table, joined, pad, shifted, result):
+    load_table(pieces, table)
     fill_padded(ids, table, place, joined, pad)
     shift_copies(pad, shifted)
     convolve(shifted, weights, result)
     grad_in[...] = (cotangent[...].astype(F32) + result[...].T).astype(BF16)
 
-    def keep(i, carry):
-        start = pl.multiple_of((i + 3) * WIDE, 8)
-        result[pl.ds(pl.multiple_of(i * 16, 16), 16), :] = shifted[3, pl.ds(start, 16), :]
-        return carry
-
-    lax.fori_loop(0, 16, keep, 0)
+
+def kernel_grad(dmixed, padded, fold, grad_dw, pad, shifted, result, taps):
+    result[...] = dmixed[...].astype(F32).T
     pad[...] = padded[...].astype(F32)
     shift_copies(pad, shifted)
     for a in range(7):
@@ -204,17 +249,25 @@
     return lax.ppermute(value, axis, [(i, i ^ bit) for i in range(lax.axis_size(axis))])
 
 
-def passed_along(value, axis, by):
-    length = lax.axis_size(axis)
-    pairs = [(i, i + by) for i in range(length) if 0 <= i + by < length]
-    return lax.ppermute(value, axis, pairs)
-
-
-def around(tiles):
-    return [
-        tiles if offset == 0 else passed_along(tiles, "tiles", -offset)
-        for offset in range(-REACH, REACH + 1)
-    ]
+def around(tiles, n_tiles, collective_id):
+    count, channels, pix = tiles.shape
+    anywhere = pl.BlockSpec(memory_space=pl.ANY)
+    return pl.pallas_call(
+        functools.partial(exchange, n_tiles),
+        out_shape=jax.ShapeDtypeStruct(((2 * REACH + 1) * count, channels, pix), tiles.dtype),
+        in_specs=[anywhere],
+        out_specs=anywhere,
+        scratch_shapes=[
+            pltpu.SemaphoreType.DMA,
+            pltpu.SemaphoreType.DMA((2 * REACH + 1,)),
+            pltpu.SemaphoreType.DMA((2 * REACH + 1,)),
+        ],
+        compiler_params=pltpu.CompilerParams(
+            collective_id=collective_id, has_side_effects=True
+        ),
+        cost_estimate=pl.CostEstimate(flops=0, bytes_accessed=40_000_000, transcendentals=0),
+        name="exchange",
+    )(tiles)
 
 
 def relay_tiles(x_scan, slot_owner, tile_count):
@@ -286,12 +339,12 @@
             jax.ShapeDtypeStruct((rows, PIX), BF16),
             jax.ShapeDtypeStruct((PAD_ROWS, rows), BF16),
         ),
-        in_specs=[SM] + [VM] * 9,
+        in_specs=[SM] + [VM] * 3,
         out_specs=(VM, VM),
         scratch_shapes=conv_scratch(),
         compiler_params=PARAMS,
         name="forward_conv",
-    )(ids, *around(owned), place, taps)
+    )(ids, around(owned, n_tiles, 0), place, taps)
     mixed = mixed.reshape(tile_count, channels, PIX)
     m_all = [mixed] + [xor_pass(mixed, "chan", k) for k in (1, 2, 3)]
 
@@ -323,7 +376,19 @@
         inv * (dnormed * gain_float - grad_sum[:, None, :] - xhat * grad_dot[:, None, :])
     ).astype(BF16)
 
-    pieces = around(dmixed)
+    steps = [1 << s for s in range(n_tiles.bit_length() - 1)]
+    grad_dw = pl.pallas_call(
+        kernel_grad,
+        out_shape=jax.ShapeDtypeStruct((56, channels), F32),
+        in_specs=[VM] * 3,
+        out_specs=VM,
+        scratch_shapes=conv_scratch()[2:] + [pltpu.VMEM((56, rows), F32)],
+        compiler_params=PARAMS,
+        name="kernel_grad",
+    )(dmixed.reshape(rows, PIX), padded, fold)
+    for bit in steps:
+        grad_dw = grad_dw + xor_pass(grad_dw, "tiles", bit)
+    pieces = around(dmixed, n_tiles, 1)
 
     fwd = [part_out[0]] + [xor_pass(part_out[k], "chan", k) for k in (1, 2, 3)]
     branch = sum(b.astype(F32) for b in fwd[1:]) + fwd[0].astype(F32)
@@ -331,7 +396,6 @@
     output = (owned.astype(F32) + scale_col * branch).astype(BF16)
 
     weights_sum = raw
-    steps = [1 << s for s in range(n_tiles.bit_length() - 1)]
     for bit in steps:
         other = xor_pass(weights_sum, "tiles", bit)
         exact = weights_sum.astype(F32) + other.astype(F32)
@@ -342,20 +406,15 @@
     grad_w1 = exact[:4].reshape(CHANNEL_COUNT, hidden) * factor
     grad_w2 = (exact[4:].reshape(CHANNEL_COUNT, hidden) * factor).T
 
-    grad_in, grad_dw = pl.pallas_call(
+    grad_in = pl.pallas_call(
         backward_conv,
-        out_shape=(
-            jax.ShapeDtypeStruct((rows, PIX), BF16),
-            jax.ShapeDtypeStruct((56, channels), F32),
-        ),
-        in_specs=[SM] + [VM] * 12,
-        out_specs=(VM, VM),
-        scratch_shapes=conv_scratch() + [pltpu.VMEM((56, rows), F32)],
+        out_shape=jax.ShapeDtypeStruct((rows, PIX), BF16),
+        in_specs=[SM] + [VM] * 4,
+        out_specs=VM,
+        scratch_shapes=conv_scratch(),
         compiler_params=PARAMS,
         name="backward_conv",
-    )(ids, *pieces, place, taps_back, padded, cotangent.reshape(rows, PIX), fold)
-    for bit in steps:
-        grad_dw = grad_dw + xor_pass(grad_dw, "tiles", bit)
+    )(ids, pieces, place, taps_back, cotangent.reshape(rows, PIX))
     grad_dw = grad_dw[:49].T * factor
     return (output, grad_in.reshape(tile_count, channels, PIX), grad_dw, grad_w1, grad_w2)
 

time: 135 us -> 123 us (0.911)
  waiting for transfers between devices: 51.6 us -> 22.1 us
  Pallas kernels: 17.9 us -> 44.5 us
  starting transfers between devices: 48.2 us -> 36.1 us
  local copies, waits for them, and re-layouts: 9.15 us -> 13 us
    pallas_call x1 -> x4, Pallas kernels: 8.57 us -> 35.2 us  [the longest x2 26.4 us: around(): pl.pallas_call(functools.partial(exchange, n_tiles), out_shape=jax.ShapeD...]
    ppermute x12 -> x0, starting transfers between devices: 25 us -> none  [passed_along(): return lax.ppermute(value, axis, pairs)]
    ppermute x12 -> x0, waiting for transfers between devices: 22.1 us -> none  [passed_along(): return lax.ppermute(value, axis, pairs)]
    ppermute x20, starting transfers between devices: 23.2 us -> 36.1 us  [xor_pass(): lax.ppermute(value, axis, [(i, i ^ bit) for i in range(lax.axis_size(axis...]
    ppermute x20, waiting for transfers between devices: 29.5 us -> 22.1 us  [xor_pass(): lax.ppermute(value, axis, [(i, i ^ bit) for i in range(lax.axis_size(axis...]
    unnamed x26 -> x28, local copies, waits for them, and re-layouts: 2.45 us -> 3.52 us
  transfers between devices with their start and end apart: 32 -> 20, of which waited for: 16 -> 7; matrix products, arithmetic and copies ran while one was open for 7% -> 10% of each run, Pallas kernels for 10% -> 33%
where the time goes in v2:
time: 123 us
  Pallas kernels  44.5 us (36%)
  starting transfers between devices  36.1 us (29%)
  waiting for transfers between devices  22.1 us (18%)
  local copies, waits for them, and re-layouts  13 us (11%)
  other arithmetic  5.85 us (5%)
    ppermute x20, starting transfers between devices, xor_pass(): lax.ppermute(value, axis, [(i, i ^ bit) for i in range(lax.axis_size(axis...  36.1 us
    pallas_call x2, Pallas kernels, around(): pl.pallas_call(functools.partial(exchange, n_tiles), out_shape=jax.ShapeD...  26.4 us
    ppermute x20, waiting for transfers between devices, xor_pass(): lax.ppermute(value, axis, [(i, i ^ bit) for i in range(lax.axis_size(axis...  22.1 us
    pallas_call x1, Pallas kernels, body(): pl.pallas_call(backward_conv, out_shape=jax.ShapeDtypeStruct((rows, PIX),...  5.52 us
    pallas_call x1, Pallas kernels, body(): pl.pallas_call(forward_conv, out_shape=(jax.ShapeDtypeStruct((rows, PIX),...  4.84 us
    pallas_call x1, Pallas kernels, body(): pl.pallas_call(mlp, out_shape=(jax.ShapeDtypeStruct((4, tile_count, chann...  4.41 us
    unnamed x28, local copies, waits for them, and re-layouts  3.52 us
    pallas_call x1, Pallas kernels, body(): pl.pallas_call(kernel_grad, out_shape=jax.ShapeDtypeStruct((56, channels)...  3.25 us
  transfers between devices with their start and end apart: 20, of which 7 were waited for; matrix products, arithmetic and copies ran while one was open for 10% of the time, Pallas kernels for 33%

profile of v2, /device:TPU:0, one launch (start us, length us, event | category | flops | bytes accessed | tf_op | source)
XLA Modules:
  0.0 122.6 jit_solution(1100070314745318204)
XLA Ops:
  0.7 1.1 multiply_convert_fusion
  1.8 0.7 broadcast_in_dim.93
  2.5 0.5 collective-permute-start.5
  3.0 2.6 %collective-permute-start.6 = (bf16[9,48,256]{2,1,0:T(8,128)(2,1)S(1)}, bf16[9,48,256]{2,1,0:T(8,128)(2,1)S(1)}, u32[]{:S(2)}, u32[]{:S(2)}) collective-permute-start(bf16[9,48,256]{2,1,0:T(8,128)(2,1)S(1)} %pad_maximum_fusion.1.d0), channel_id=1, source_target_pairs={{0,2},{1,3},{2,0},{3,1},{4,6},{5,7},{6,4},{7,5},{8,10},{9,11},{10,... | collective-permute-start | bytes 663560 | tf_op jit(solution)/shard_map/ppermute | solution.py:249
  5.7 0.7 and_select_fusion.1
  6.3 0.7 broadcast_compare_fusion
  7.3 0.2 fusion.12
  7.6 1.8 %collective-permute-start.1 = (s32[4]{0:T(128)S(1)}, s32[4]{0:T(128)S(1)}, u32[]{:S(2)}, u32[]{:S(2)}) collective-permute-start(s32[4]{0:T(128)S(1)} %broadcast_select_fusion), channel_id=1, source_target_pairs={{0,4},{4,0},{8,12},{12,8},{16,20},{20,16},{24,28},{28,24},{1,5},{5... | collective-permute-start | bytes 56 | tf_op jit(solution)/shard_map/ppermute | solution.py:249
  9.4 1.5 %gather_fusion = bf16[4,48,256]{2,1,0:T(8,128)(2,1)S(1)} fusion(bf16[16,48,256]{2,1,0:T(8,128)(2,1)} %param.12, s32[1024]{0:T(1024)S(1)} %pad_clamp_fusion.2), kind=kCustom, calls=%fused_computation | custom fusion | bytes 196624 | tf_op jit(solution)/shard_map/jit(_take)/gather | solution.py:290
  11.0 0.3 collective-permute-start
  11.3 0.7 convert_element_type.99
  12.1 0.8 rev.3
  12.9 0.8 copy.34
  14.2 1.6 %collective-permute-done = bf16[4,48,256]{2,1,0:T(8,128)(2,1)S(1)} collective-permute-done((bf16[4,48,256]{2,1,0:T(8,128)(2,1)S(1)}, bf16[4,48,256]{2,1,0:T(8,128)(2,1)S(1)}, u32[]{:S(2)}, u32[]{:S(2)}) %collective-permute-start) | collective-permute-done | bytes 98336 | tf_op jit(solution)/shard_map/ppermute | solution.py:249
  15.9 1.2 %gather_fusion.1 = bf16[8,48,256]{2,1,0:T(8,128)(2,1)} fusion(bf16[20,48,256]{2,1,0:T(8,128)(2,1)S(1)} %pad_maximum_fusion, s32[1024]{0:T(1024)S(1)} %pad_clamp_fusion.1), kind=kCustom, calls=%fused_computation.1 | custom fusion | bytes 393248 | tf_op jit(solution)/shard_map/jit(_take)/gather | solution.py:299
  17.1 13.6 %exchange.2.pieces = bf16[56,48,256]{2,1,0:T(8,128)(2,1)} custom-call(bf16[8,48,256]{2,1,0:T(8,128)(2,1)} %gather_fusion.1), custom_call_target="tpu_custom_call" | custom-call | bytes 40000000 | tf_op jit(solution)/shard_map/exchange/pallas_call | solution.py:255
  30.8 1.3 %copy-done.2 = bf16[56,48,256]{2,1,0:T(8,128)(2,1)S(1)} copy-done((bf16[56,48,256]{2,1,0:T(8,128)(2,1)S(1)}, bf16[56,48,256]{2,1,0:T(8,128)(2,1)}, u32[]{:S(2)}) %copy-start.2) | copy-done | bytes 1376280
  32.1 4.8 %forward_conv.1 = (bf16[384,256]{1,0:T(8,128)(2,1)S(1)}, bf16[544,384]{1,0:T(8,128)(2,1)S(1)}) custom-call(s32[8,8]{1,0:T(8,128)S(1)} %and_select_fusion.ids, bf16[56,48,256]{2,1,0:T(8,128)(2,1)S(1)} %copy-done.2, bf16[544,1024]{1,0:T(8,128)(2,1)S(1)} %copy-done.3, f32[49,384]{1,0:T(8,128)S(1)} %tile.9.weights), custom_call_target="tpu_custom_call" | custom-call | tf_op jit(solution)/shard_map/forward_conv/pallas_call | solution.py:336
  37.0 1.6 %collective-permute-start.3 = (bf16[8,48,256]{2,1,0:T(8,128)(2,1)S(1)}, bf16[8,48,256]{2,1,0:T(8,128)(2,1)}, u32[]{:S(2)}, u32[]{:S(2)}) collective-permute-start(bf16[8,48,256]{2,1,0:T(8,128)(2,1)S(1)} %bitcast.59), channel_id=1, source_target_pairs={{0,2},{1,3},{2,0},{3,1},{4,6},{5,7},{6,4},{7,5},{8,10},{9,11},{10,... | collective-permute-start | bytes 589832 | tf_op jit(solution)/shard_map/ppermute | solution.py:249
  38.6 0.3 collective-permute-start.4
  38.9 0.6 gather_fusion.3
  39.6 0.6 gather_fusion.2
  40.5 0.7 tile.20
  41.2 1.0 tile.21.weights
  42.3 2.6 %collective-permute-done.3.m2 = bf16[8,48,256]{2,1,0:T(8,128)(2,1)} collective-permute-done((bf16[8,48,256]{2,1,0:T(8,128)(2,1)S(1)}, bf16[8,48,256]{2,1,0:T(8,128)(2,1)}, u32[]{:S(2)}, u32[]{:S(2)}) %collective-permute-start.3) | collective-permute-done | bytes 196640 | tf_op jit(solution)/shard_map/ppermute | solution.py:249
  44.9 3.3 %collective-permute-done.4.m3 = bf16[8,48,256]{2,1,0:T(8,128)(2,1)} collective-permute-done((bf16[8,48,256]{2,1,0:T(8,128)(2,1)S(1)}, bf16[8,48,256]{2,1,0:T(8,128)(2,1)}, u32[]{:S(2)}, u32[]{:S(2)}) %collective-permute-start.4) | collective-permute-done | bytes 196640 | tf_op jit(solution)/shard_map/ppermute | solution.py:249
  48.2 4.4 %mlp.1 = (bf16[4,8,48,256]{3,2,1,0:T(8,128)(2,1)S(1)}, bf16[4,9,48,256]{3,2,1,0:T(8,128)(2,1)S(1)}, bf16[8,48,192]{2,1,0:T(8,128)(2,1)S(1)}, f32[2,8,256]{2,1,0:T(8,128)S(1)}) custom-call(s32[4]{0:T(128)S(1)} %iota_xor_fusion.perm, bf16[8,48,256]{2,1,0:T(8,128)(2,1)S(1)} %bitcast.61, bf16[8,48,256]{2,1,0:T(8,128)(2,1)S(1)} %collective-permute-done.2.m1, ...), custom_call_target="tpu_custom_call" | custom-call | tf_op jit(solution)/shard_map/mlp/pallas_call | solution.py:352
  52.6 4.1 %collective-permute-start.17 = (bf16[8,48,192]{2,1,0:T(8,128)(2,1)S(1)}, bf16[8,48,192]{2,1,0:T(8,128)(2,1)S(1)}, u32[]{:S(2)}, u32[]{:S(2)}) collective-permute-start(bf16[8,48,192]{2,1,0:T(8,128)(2,1)S(1)} %get-tuple-element.16), channel_id=1, source_target_pairs={{0,4},{4,0},{8,12},{12,8},{16,20},{20,16},{24,28},{28,24},{1,5},{5... | collective-permute-start | bytes 442376 | tf_op jit(solution)/shard_map/ppermute | solution.py:249
  56.9 1.6 %collective-permute-start.12 = (bf16[9,48,256]{2,1,0:T(8,128)(2,1)S(1)}, bf16[9,48,256]{2,1,0:T(8,128)(2,1)S(1)}, u32[]{:S(2)}, u32[]{:S(2)}) collective-permute-start(bf16[9,48,256]{2,1,0:T(8,128)(2,1)S(1)} %get-tuple-element.42), channel_id=1, source_target_pairs={{0,2},{1,3},{2,0},{3,1},{4,6},{5,7},{6,4},{7,5},{8,10},{9,11},{10,... | collective-permute-start | bytes 663560 | tf_op jit(solution)/shard_map/ppermute | solution.py:249
  58.4 0.3 collective-permute-start.13
  58.8 1.5 %collective-permute-start.10 = (bf16[8,48,256]{2,1,0:T(8,128)(2,1)S(1)}, bf16[8,48,256]{2,1,0:T(8,128)(2,1)S(1)}, u32[]{:S(2)}, u32[]{:S(2)}) collective-permute-start(bf16[8,48,256]{2,1,0:T(8,128)(2,1)S(1)} %get-tuple-element.44), channel_id=1, source_target_pairs={{0,3},{1,2},{2,1},{3,0},{4,7},{5,6},{6,5},{7,4},{8,11},{9,10},{10,... | collective-permute-start | bytes 589832 | tf_op jit(solution)/shard_map/ppermute | solution.py:249
  60.5 4.7 %collective-permute-done.12 = bf16[9,48,256]{2,1,0:T(8,128)(2,1)S(1)} collective-permute-done((bf16[9,48,256]{2,1,0:T(8,128)(2,1)S(1)}, bf16[9,48,256]{2,1,0:T(8,128)(2,1)S(1)}, u32[]{:S(2)}, u32[]{:S(2)}) %collective-permute-start.12) | collective-permute-done | bytes 221216 | tf_op jit(solution)/shard_map/ppermute | solution.py:249
  65.2 1.5 %collective-permute-start.9 = (bf16[8,48,256]{2,1,0:T(8,128)(2,1)S(1)}, bf16[8,48,256]{2,1,0:T(8,128)(2,1)S(1)}, u32[]{:S(2)}, u32[]{:S(2)}) collective-permute-start(bf16[8,48,256]{2,1,0:T(8,128)(2,1)S(1)} %get-tuple-element.45), channel_id=1, source_target_pairs={{0,2},{1,3},{2,0},{3,1},{4,6},{5,7},{6,4},{7,5},{8,10},{9,11},{10,... | collective-permute-start | bytes 589832 | tf_op jit(solution)/shard_map/ppermute | solution.py:249
  66.7 2.3 %collective-permute-done.13 = bf16[9,48,256]{2,1,0:T(8,128)(2,1)S(1)} collective-permute-done((bf16[9,48,256]{2,1,0:T(8,128)(2,1)S(1)}, bf16[9,48,256]{2,1,0:T(8,128)(2,1)S(1)}, u32[]{:S(2)}, u32[]{:S(2)}) %collective-permute-start.13) | collective-permute-done | bytes 221216 | tf_op jit(solution)/shard_map/ppermute | solution.py:249
  69.3 3.2 %kernel_grad.1 = f32[56,48]{1,0:T(8,128)S(1)} custom-call(bf16[384,256]{1,0:T(8,128)(2,1)S(1)} %bitcast.52, bf16[544,384]{1,0:T(8,128)(2,1)S(1)} %get-tuple-element.15.padded, f32[384,48]{1,0:T(8,128)S(1)} %copy-done.6), custom_call_target="tpu_custom_call" | custom-call | tf_op jit(solution)/shard_map/kernel_grad/pallas_call | solution.py:380
  72.6 0.2 collective-permute-start.14
  72.9 5.8 %collective-permute-start.18 = (bf16[8,48,192]{2,1,0:T(8,128)(2,1)S(1)}, bf16[8,48,192]{2,1,0:T(8,128)(2,1)S(1)}, u32[]{:S(2)}, u32[]{:S(2)}) collective-permute-start(bf16[8,48,192]{2,1,0:T(8,128)(2,1)S(1)} %reduce-precision_convert_fusion.1), channel_id=1, source_target_pairs={{0,8},{4,12},{8,0},{12,4},{16,24},{20,28},{24,16},{28,20},{1,9},{5... | collective-permute-start | bytes 442376 | tf_op jit(solution)/shard_map/ppermute | solution.py:249
  78.7 3.9 %collective-permute-start.15 = (f32[56,48]{1,0:T(8,128)S(1)}, f32[56,48]{1,0:T(8,128)S(1)}, u32[]{:S(2)}, u32[]{:S(2)}) collective-permute-start(f32[56,48]{1,0:T(8,128)S(1)} %add.99), channel_id=1, source_target_pairs={{0,8},{4,12},{8,0},{12,4},{16,24},{20,28},{24,16},{28,20},{1,9},{5... | collective-permute-start | bytes 32264 | tf_op jit(solution)/shard_map/ppermute | solution.py:249
  82.6 0.8 add_convert_fusion
  83.4 12.8 %exchange.3.pieces = bf16[56,48,256]{2,1,0:T(8,128)(2,1)} custom-call(bf16[8,48,256]{2,1,0:T(8,128)(2,1)} %copy-done.4), custom_call_target="tpu_custom_call" | custom-call | bytes 40000000 | tf_op jit(solution)/shard_map/exchange/pallas_call | solution.py:255
  96.3 1.3 %copy-done.1 = bf16[56,48,256]{2,1,0:T(8,128)(2,1)S(1)} copy-done((bf16[56,48,256]{2,1,0:T(8,128)(2,1)S(1)}, bf16[56,48,256]{2,1,0:T(8,128)(2,1)}, u32[]{:S(2)}) %copy-start.1) | copy-done | bytes 1376280
  97.6 5.5 %backward_conv.1 = bf16[384,256]{1,0:T(8,128)(2,1)} custom-call(s32[8,8]{1,0:T(8,128)S(1)} %and_select_fusion.ids, bf16[56,48,256]{2,1,0:T(8,128)(2,1)S(1)} %copy-done.1, bf16[544,1024]{1,0:T(8,128)(2,1)S(1)} %copy-done.3, f32[49,384]{1,0:T(8,128)S(1)} %tile.21.weights, bf16[384,256]{1,0:T(8,128)(2,1)S(1)} %bitcast.57), custom_call_target="tpu_custom_call" | custom-call | tf_op jit(solution)/shard_map/backward_conv/pallas_call | solution.py:409
  103.1 9.6 %collective-permute-start.16 = (f32[56,48]{1,0:T(8,128)S(1)}, f32[56,48]{1,0:T(8,128)S(1)}, u32[]{:S(2)}, u32[]{:S(2)}) collective-permute-start(f32[56,48]{1,0:T(8,128)S(1)} %add.100), channel_id=1, source_target_pairs={{0,16},{4,20},{8,24},{12,28},{16,0},{20,4},{24,8},{28,12},{1,17},{... | collective-permute-start | bytes 32264 | tf_op jit(solution)/shard_map/ppermute | solution.py:249
  112.9 4.0 %collective-permute-done.16 = f32[56,48]{1,0:T(8,128)S(1)} collective-permute-done((f32[56,48]{1,0:T(8,128)S(1)}, f32[56,48]{1,0:T(8,128)S(1)}, u32[]{:S(2)}, u32[]{:S(2)}) %collective-permute-start.16) | collective-permute-done | bytes 10784 | tf_op jit(solution)/shard_map/ppermute | solution.py:249
  117.0 0.7 copy.41
  117.7 3.4 %collective-permute-done.19 = bf16[8,48,192]{2,1,0:T(8,128)(2,1)S(1)} collective-permute-done((bf16[8,48,192]{2,1,0:T(8,128)(2,1)S(1)}, bf16[8,48,192]{2,1,0:T(8,128)(2,1)S(1)}, u32[]{:S(2)}, u32[]{:S(2)}) %collective-permute-start.19) | collective-permute-done | bytes 147488 | tf_op jit(solution)/shard_map/ppermute | solution.py:249
  121.1 0.7 slice_multiply_fusion.1
  121.8 0.8 copy.40
  (81 shorter events, 2.4 us)
Async XLA Ops:
  0.6 38.9 %copy-start = (bf16[192,192]{1,0:T(8,128)(2,1)S(1)}, bf16[192,192]{1,0:T(8,128)(2,1)}, u32[]{:S(2)}) copy-start(bf16[192,192]{1,0:T(8,128)(2,1)} %param.18) | copy-start | bytes 221188
  0.6 15.2 %copy-start.8 = (bf16[16,48,256]{2,1,0:T(8,128)(2,1)S(1)}, bf16[16,48,256]{2,1,0:T(8,128)(2,1)}, u32[]{:S(2)}) copy-start(bf16[16,48,256]{2,1,0:T(8,128)(2,1)} %param.12) | copy-start | bytes 1179652
  0.7 13.3 %copy-start.9 = (bf16[192,192]{1,0:T(8,128)(2,1)S(1)}, bf16[192,192]{1,0:T(8,128)(2,1)}, u32[]{:S(2)}) copy-start(bf16[192,192]{1,0:T(8,128)(2,1)} %param.20) | copy-start | bytes 221188
  0.7 13.4 %copy-start.10 = (s32[8,8]{1,0:T(8,128)S(1)}, s32[8,8]{1,0:T(8,128)}, u32[]{:S(2)}) copy-start(s32[8,8]{1,0:T(8,128)} %param.14) | copy-start | bytes 772
  2.5 36.1 %collective-permute-start.5 = (bf16[9,48,256]{2,1,0:T(8,128)(2,1)S(1)}, bf16[9,48,256]{2,1,0:T(8,128)(2,1)S(1)}, u32[]{:S(2)}, u32[]{:S(2)}) collective-permute-start(bf16[9,48,256]{2,1,0:T(8,128)(2,1)S(1)} %pad_maximum_fusion.1.d0), channel_id=1, source_target_pairs={{0,1},{1,0},{2,3},{3,2},{4,5},{5,4},{6,7},{7,6},{8,9},{9,8},{10,11... | collective-permute-start | bytes 663560 | tf_op jit(solution)/shard_map/ppermute | solution.py:249
  3.0 39.2 %collective-permute-start.6 = (bf16[9,48,256]{2,1,0:T(8,128)(2,1)S(1)}, bf16[9,48,256]{2,1,0:T(8,128)(2,1)S(1)}, u32[]{:S(2)}, u32[]{:S(2)}) collective-permute-start(bf16[9,48,256]{2,1,0:T(8,128)(2,1)S(1)} %pad_maximum_fusion.1.d0), channel_id=1, source_target_pairs={{0,2},{1,3},{2,0},{3,1},{4,6},{5,7},{6,4},{7,5},{8,10},{9,11},{10,... | collective-permute-start | bytes 663560 | tf_op jit(solution)/shard_map/ppermute | solution.py:249
  5.6 36.7 %collective-permute-start.7 = (bf16[9,48,256]{2,1,0:T(8,128)(2,1)S(1)}, bf16[9,48,256]{2,1,0:T(8,128)(2,1)S(1)}, u32[]{:S(2)}, u32[]{:S(2)}) collective-permute-start(bf16[9,48,256]{2,1,0:T(8,128)(2,1)S(1)} %pad_maximum_fusion.1.d0), channel_id=1, source_target_pairs={{0,3},{1,2},{2,1},{3,0},{4,7},{5,6},{6,5},{7,4},{8,11},{9,10},{10,... | collective-permute-start | bytes 663560 | tf_op jit(solution)/shard_map/ppermute | solution.py:249
  7.6 6.4 %collective-permute-start.1 = (s32[4]{0:T(128)S(1)}, s32[4]{0:T(128)S(1)}, u32[]{:S(2)}, u32[]{:S(2)}) collective-permute-start(s32[4]{0:T(128)S(1)} %broadcast_select_fusion), channel_id=1, source_target_pairs={{0,4},{4,0},{8,12},{12,8},{16,20},{20,16},{24,28},{28,24},{1,5},{5... | collective-permute-start | bytes 56 | tf_op jit(solution)/shard_map/ppermute | solution.py:249
  11.0 4.8 %collective-permute-start = (bf16[4,48,256]{2,1,0:T(8,128)(2,1)S(1)}, bf16[4,48,256]{2,1,0:T(8,128)(2,1)S(1)}, u32[]{:S(2)}, u32[]{:S(2)}) collective-permute-start(bf16[4,48,256]{2,1,0:T(8,128)(2,1)S(1)} %gather_fusion), channel_id=1, source_target_pairs={{0,4},{4,0},{8,12},{12,8},{16,20},{20,16},{24,28},{28,24},{1,5},{5... | collective-permute-start | bytes 294920 | tf_op jit(solution)/shard_map/ppermute | solution.py:249
  14.2 16.6 %copy-start.3 = (bf16[544,1024]{1,0:T(8,128)(2,1)S(1)}, bf16[544,1024]{1,0:T(8,128)(2,1)}, u32[]{:S(2)}) copy-start(bf16[544,1024]{1,0:T(8,128)(2,1)} %constant.68.clone.place) | copy-start | bytes 3342340
  30.8 1.3 %copy-start.2 = (bf16[56,48,256]{2,1,0:T(8,128)(2,1)S(1)}, bf16[56,48,256]{2,1,0:T(8,128)(2,1)}, u32[]{:S(2)}) copy-start(bf16[56,48,256]{2,1,0:T(8,128)(2,1)} %exchange.2.pieces) | copy-start | bytes 4128772
  32.1 8.1 %copy-start.12 = (bf16[192]{0:T(256)(128)(2,1)S(1)}, bf16[192]{0:T(256)(128)(2,1)}, u32[]{:S(2)}) copy-start(bf16[192]{0:T(256)(128)(2,1)} %param.19) | copy-start | bytes 1156
  37.0 5.3 %collective-permute-start.2 = (bf16[8,48,256]{2,1,0:T(8,128)(2,1)S(1)}, bf16[8,48,256]{2,1,0:T(8,128)(2,1)S(1)}, u32[]{:S(2)}, u32[]{:S(2)}) collective-permute-start(bf16[8,48,256]{2,1,0:T(8,128)(2,1)S(1)} %bitcast.58), channel_id=1, source_target_pairs={{0,1},{1,0},{2,3},{3,2},{4,5},{5,4},{6,7},{7,6},{8,9},{9,8},{10,11... | collective-permute-start | bytes 589832 | tf_op jit(solution)/shard_map/ppermute | solution.py:249
  37.0 7.9 %collective-permute-start.3 = (bf16[8,48,256]{2,1,0:T(8,128)(2,1)S(1)}, bf16[8,48,256]{2,1,0:T(8,128)(2,1)}, u32[]{:S(2)}, u32[]{:S(2)}) collective-permute-start(bf16[8,48,256]{2,1,0:T(8,128)(2,1)S(1)} %bitcast.59), channel_id=1, source_target_pairs={{0,2},{1,3},{2,0},{3,1},{4,6},{5,7},{6,4},{7,5},{8,10},{9,11},{10,... | collective-permute-start | bytes 589832 | tf_op jit(solution)/shard_map/ppermute | solution.py:249
  38.6 9.6 %collective-permute-start.4 = (bf16[8,48,256]{2,1,0:T(8,128)(2,1)S(1)}, bf16[8,48,256]{2,1,0:T(8,128)(2,1)}, u32[]{:S(2)}, u32[]{:S(2)}) collective-permute-start(bf16[8,48,256]{2,1,0:T(8,128)(2,1)S(1)} %bitcast.60), channel_id=1, source_target_pairs={{0,3},{1,2},{2,1},{3,0},{4,7},{5,6},{6,5},{7,4},{8,11},{9,10},{10,... | collective-permute-start | bytes 589832 | tf_op jit(solution)/shard_map/ppermute | solution.py:249
  52.6 20.2 %collective-permute-start.17 = (bf16[8,48,192]{2,1,0:T(8,128)(2,1)S(1)}, bf16[8,48,192]{2,1,0:T(8,128)(2,1)S(1)}, u32[]{:S(2)}, u32[]{:S(2)}) collective-permute-start(bf16[8,48,192]{2,1,0:T(8,128)(2,1)S(1)} %get-tuple-element.16), channel_id=1, source_target_pairs={{0,4},{4,0},{8,12},{12,8},{16,20},{20,16},{24,28},{28,24},{1,5},{5... | collective-permute-start | bytes 442376 | tf_op jit(solution)/shard_map/ppermute | solution.py:249
  56.8 3.5 %collective-permute-start.11 = (bf16[9,48,256]{2,1,0:T(8,128)(2,1)S(1)}, bf16[9,48,256]{2,1,0:T(8,128)(2,1)S(1)}, u32[]{:S(2)}, u32[]{:S(2)}) collective-permute-start(bf16[9,48,256]{2,1,0:T(8,128)(2,1)S(1)} %get-tuple-element.40), channel_id=1, source_target_pairs={{0,1},{1,0},{2,3},{3,2},{4,5},{5,4},{6,7},{7,6},{8,9},{9,8},{10,11... | collective-permute-start | bytes 663560 | tf_op jit(solution)/shard_map/ppermute | solution.py:249
  56.9 8.3 %collective-permute-start.12 = (bf16[9,48,256]{2,1,0:T(8,128)(2,1)S(1)}, bf16[9,48,256]{2,1,0:T(8,128)(2,1)S(1)}, u32[]{:S(2)}, u32[]{:S(2)}) collective-permute-start(bf16[9,48,256]{2,1,0:T(8,128)(2,1)S(1)} %get-tuple-element.42), channel_id=1, source_target_pairs={{0,2},{1,3},{2,0},{3,1},{4,6},{5,7},{6,4},{7,5},{8,10},{9,11},{10,... | collective-permute-start | bytes 663560 | tf_op jit(solution)/shard_map/ppermute | solution.py:249
  58.4 10.6 %collective-permute-start.13 = (bf16[9,48,256]{2,1,0:T(8,128)(2,1)S(1)}, bf16[9,48,256]{2,1,0:T(8,128)(2,1)S(1)}, u32[]{:S(2)}, u32[]{:S(2)}) collective-permute-start(bf16[9,48,256]{2,1,0:T(8,128)(2,1)S(1)} %get-tuple-element.41), channel_id=1, source_target_pairs={{0,3},{1,2},{2,1},{3,0},{4,7},{5,6},{6,5},{7,4},{8,11},{9,10},{10,... | collective-permute-start | bytes 663560 | tf_op jit(solution)/shard_map/ppermute | solution.py:249
  58.8 10.5 %copy-start.6 = (f32[384,48]{1,0:T(8,128)S(1)}, f32[384,48]{1,0:T(8,128)}, u32[]{:S(2)}) copy-start(f32[384,48]{1,0:T(8,128)} %constant.69.clone.fold) | copy-start | bytes 221188
  58.8 23.8 %collective-permute-start.10 = (bf16[8,48,256]{2,1,0:T(8,128)(2,1)S(1)}, bf16[8,48,256]{2,1,0:T(8,128)(2,1)S(1)}, u32[]{:S(2)}, u32[]{:S(2)}) collective-permute-start(bf16[8,48,256]{2,1,0:T(8,128)(2,1)S(1)} %get-tuple-element.44), channel_id=1, source_target_pairs={{0,3},{1,2},{2,1},{3,0},{4,7},{5,6},{6,5},{7,4},{8,11},{9,10},{10,... | collective-permute-start | bytes 589832 | tf_op jit(solution)/shard_map/ppermute | solution.py:249
  60.3 22.3 %collective-permute-start.8 = (bf16[8,48,256]{2,1,0:T(8,128)(2,1)S(1)}, bf16[8,48,256]{2,1,0:T(8,128)(2,1)S(1)}, u32[]{:S(2)}, u32[]{:S(2)}) collective-permute-start(bf16[8,48,256]{2,1,0:T(8,128)(2,1)S(1)} %get-tuple-element.43), channel_id=1, source_target_pairs={{0,1},{1,0},{2,3},{3,2},{4,5},{5,4},{6,7},{7,6},{8,9},{9,8},{10,11... | collective-permute-start | bytes 589832 | tf_op jit(solution)/shard_map/ppermute | solution.py:249
  65.2 17.4 %collective-permute-start.9 = (bf16[8,48,256]{2,1,0:T(8,128)(2,1)S(1)}, bf16[8,48,256]{2,1,0:T(8,128)(2,1)S(1)}, u32[]{:S(2)}, u32[]{:S(2)}) collective-permute-start(bf16[8,48,256]{2,1,0:T(8,128)(2,1)S(1)} %get-tuple-element.45), channel_id=1, source_target_pairs={{0,2},{1,3},{2,0},{3,1},{4,6},{5,7},{6,4},{7,5},{8,10},{9,11},{10,... | collective-permute-start | bytes 589832 | tf_op jit(solution)/shard_map/ppermute | solution.py:249
  69.1 13.5 %copy-start.7 = (bf16[8,48,256]{2,1,0:T(8,128)(2,1)S(1)}, bf16[8,48,256]{2,1,0:T(8,128)(2,1)}, u32[]{:S(2)}) copy-start(bf16[8,48,256]{2,1,0:T(8,128)(2,1)} %gather_fusion.1) | copy-start | bytes 589828
  69.1 13.5 %copy-start.11 = (f32[48]{0:T(128)S(1)}, f32[48]{0:T(128)}, u32[]{:S(2)}) copy-start(f32[48]{0:T(128)} %param.21) | copy-start | bytes 580
  69.3 14.1 %copy-start.4 = (bf16[8,48,256]{2,1,0:T(8,128)(2,1)}, bf16[8,48,256]{2,1,0:T(8,128)(2,1)S(1)}, u32[]{:S(2)}) copy-start(bf16[8,48,256]{2,1,0:T(8,128)(2,1)S(1)} %fusion.3.own) | copy-start | bytes 589828
  72.6 6.1 %collective-permute-start.14 = (f32[56,48]{1,0:T(8,128)S(1)}, f32[56,48]{1,0:T(8,128)S(1)}, u32[]{:S(2)}, u32[]{:S(2)}) collective-permute-start(f32[56,48]{1,0:T(8,128)S(1)} %kernel_grad.1), channel_id=1, source_target_pairs={{0,4},{4,0},{8,12},{12,8},{16,20},{20,16},{24,28},{28,24},{1,5},{5... | collective-permute-start | bytes 32264 | tf_op jit(solution)/shard_map/ppermute | solution.py:249
  72.9 39.9 %collective-permute-start.18 = (bf16[8,48,192]{2,1,0:T(8,128)(2,1)S(1)}, bf16[8,48,192]{2,1,0:T(8,128)(2,1)S(1)}, u32[]{:S(2)}, u32[]{:S(2)}) collective-permute-start(bf16[8,48,192]{2,1,0:T(8,128)(2,1)S(1)} %reduce-precision_convert_fusion.1), channel_id=1, source_target_pairs={{0,8},{4,12},{8,0},{12,4},{16,24},{20,28},{24,16},{28,20},{1,9},{5... | collective-permute-start | bytes 442376 | tf_op jit(solution)/shard_map/ppermute | solution.py:249
  78.7 17.6 %copy-start.5 = (bf16[8,48,256]{2,1,0:T(8,128)(2,1)S(1)}, bf16[8,48,256]{2,1,0:T(8,128)(2,1)}, u32[]{:S(2)}) copy-start(bf16[8,48,256]{2,1,0:T(8,128)(2,1)} %param.15) | copy-start | bytes 589828
  78.7 24.5 %collective-permute-start.15 = (f32[56,48]{1,0:T(8,128)S(1)}, f32[56,48]{1,0:T(8,128)S(1)}, u32[]{:S(2)}, u32[]{:S(2)}) collective-permute-start(f32[56,48]{1,0:T(8,128)S(1)} %add.99), channel_id=1, source_target_pairs={{0,8},{4,12},{8,0},{12,4},{16,24},{20,28},{24,16},{28,20},{1,9},{5... | collective-permute-start | bytes 32264 | tf_op jit(solution)/shard_map/ppermute | solution.py:249
  96.3 1.3 %copy-start.1 = (bf16[56,48,256]{2,1,0:T(8,128)(2,1)S(1)}, bf16[56,48,256]{2,1,0:T(8,128)(2,1)}, u32[]{:S(2)}) copy-start(bf16[56,48,256]{2,1,0:T(8,128)(2,1)} %exchange.3.pieces) | copy-start | bytes 4128772
  103.1 13.8 %collective-permute-start.16 = (f32[56,48]{1,0:T(8,128)S(1)}, f32[56,48]{1,0:T(8,128)S(1)}, u32[]{:S(2)}, u32[]{:S(2)}) collective-permute-start(f32[56,48]{1,0:T(8,128)S(1)} %add.100), channel_id=1, source_target_pairs={{0,16},{4,20},{8,24},{12,28},{16,0},{20,4},{24,8},{28,12},{1,17},{... | collective-permute-start | bytes 32264 | tf_op jit(solution)/shard_map/ppermute | solution.py:249
  112.9 8.2 %collective-permute-start.19 = (bf16[8,48,192]{2,1,0:T(8,128)(2,1)S(1)}, bf16[8,48,192]{2,1,0:T(8,128)(2,1)S(1)}, u32[]{:S(2)}, u32[]{:S(2)}) collective-permute-start(bf16[8,48,192]{2,1,0:T(8,128)(2,1)S(1)} %reduce-precision_convert_fusion), channel_id=1, source_target_pairs={{0,16},{4,20},{8,24},{12,28},{16,0},{20,4},{24,8},{28,12},{1,17},{... | collective-permute-start | bytes 442376 | tf_op jit(solution)/shard_map/ppermute | solution.py:249

commit v3 on v2

--- a/solution.py
+++ b/solution.py
@@ -104,11 +104,18 @@
             barrier, inc=1, device_id={"tiles": me + d}, device_id_type=pl.DeviceIdType.MESH
         )
 
+    def used(slot):
+        if slot >= REACH + 2:
+            return pl.ds(0, PIX // 2)
+        if slot <= REACH - 2:
+            return pl.ds(PIX // 2, PIX // 2)
+        return pl.ds(0, PIX)
+
     def copy(d):
         slot = REACH - d
         return pltpu.make_async_remote_copy(
-            src_ref=own,
-            dst_ref=table.at[pl.ds(slot * 8, 8)],
+            src_ref=own.at[:, :, used(slot)],
+            dst_ref=table.at[pl.ds(slot * 8, 8), :, used(slot)],
             send_sem=send_sems.at[slot],
             recv_sem=recv_sems.at[slot],
             device_id={"tiles": me + d},
@@ -118,8 +125,8 @@
     def arrival(d):
         slot = REACH + d
         return pltpu.make_async_remote_copy(
-            src_ref=own,
-            dst_ref=table.at[pl.ds(slot * 8, 8)],
+            src_ref=own.at[:, :, used(slot)],
+            dst_ref=table.at[pl.ds(slot * 8, 8), :, used(slot)],
             send_sem=send_sems.at[slot],
             recv_sem=recv_sems.at[slot],
             device_id={"tiles": me + d},

time: 123 us -> 115 us (0.935)
  starting transfers between devices: 36.1 us -> 28.8 us
  Pallas kernels: 44.5 us -> 42 us
  waiting for transfers between devices: 22.1 us -> 23.7 us
    ppermute x20, starting transfers between devices: 36.1 us -> 28.8 us  [xor_pass(): lax.ppermute(value, axis, [(i, i ^ bit) for i in range(lax.axis_size(axis...]
    pallas_call x2, Pallas kernels: 26.4 us -> 24 us  [around(): pl.pallas_call(functools.partial(exchange, n_tiles), out_shape=jax.ShapeD...]
    ppermute x20, waiting for transfers between devices: 22.1 us -> 23.7 us  [xor_pass(): lax.ppermute(value, axis, [(i, i ^ bit) for i in range(lax.axis_size(axis...]
  transfers between devices with their start and end apart: 20 -> 20, of which waited for: 7 -> 8; matrix products, arithmetic and copies ran while one was open for 10% -> 11% of each run, Pallas kernels for 33% -> 33%
where the time goes in v3:
time: 115 us
  Pallas kernels  42 us (37%)
  starting transfers between devices  28.8 us (25%)
  waiting for transfers between devices  23.7 us (21%)
  local copies, waits for them, and re-layouts  13 us (11%)
  other arithmetic  5.85 us (5%)
    ppermute x20, starting transfers between devices, xor_pass(): lax.ppermute(value, axis, [(i, i ^ bit) for i in range(lax.axis_size(axis...  28.8 us
    pallas_call x2, Pallas kernels, around(): pl.pallas_call(functools.partial(exchange, n_tiles), out_shape=jax.ShapeD...  24 us
    ppermute x20, waiting for transfers between devices, xor_pass(): lax.ppermute(value, axis, [(i, i ^ bit) for i in range(lax.axis_size(axis...  23.7 us
    pallas_call x1, Pallas kernels, body(): pl.pallas_call(backward_conv, out_shape=jax.ShapeDtypeStruct((rows, PIX),...  5.51 us
    pallas_call x1, Pallas kernels, body(): pl.pallas_call(forward_conv, out_shape=(jax.ShapeDtypeStruct((rows, PIX),...  4.84 us
    pallas_call x1, Pallas kernels, body(): pl.pallas_call(mlp, out_shape=(jax.ShapeDtypeStruct((4, tile_count, chann...  4.41 us
    unnamed x28, local copies, waits for them, and re-layouts  3.52 us
    pallas_call x1, Pallas kernels, body(): pl.pallas_call(kernel_grad, out_shape=jax.ShapeDtypeStruct((56, channels)...  3.25 us
  transfers between devices with their start and end apart: 20, of which 8 were waited for; matrix products, arithmetic and copies ran while one was open for 11% of the time, Pallas kernels for 33%

profile of v3, /device:TPU:0, one launch (start us, length us, event | category | flops | bytes accessed | tf_op | source)
XLA Modules:
  0.0 114.5 jit_solution(8362712773864490939)
XLA Ops:
  0.7 1.1 multiply_convert_fusion
  1.8 0.7 broadcast_in_dim.93
  2.5 0.5 collective-permute-start.5
  3.0 2.6 %collective-permute-start.6 = (bf16[9,48,256]{2,1,0:T(8,128)(2,1)S(1)}, bf16[9,48,256]{2,1,0:T(8,128)(2,1)S(1)}, u32[]{:S(2)}, u32[]{:S(2)}) collective-permute-start(bf16[9,48,256]{2,1,0:T(8,128)(2,1)S(1)} %pad_maximum_fusion.1.d0), channel_id=1, source_target_pairs={{0,2},{1,3},{2,0},{3,1},{4,6},{5,7},{6,4},{7,5},{8,10},{9,11},{10,... | collective-permute-start | bytes 663560 | tf_op jit(solution)/shard_map/ppermute | solution.py:256
  5.7 0.7 and_select_fusion.1
  6.3 0.7 broadcast_compare_fusion
  7.3 0.2 fusion.12
  7.6 1.8 %collective-permute-start.1 = (s32[4]{0:T(128)S(1)}, s32[4]{0:T(128)S(1)}, u32[]{:S(2)}, u32[]{:S(2)}) collective-permute-start(s32[4]{0:T(128)S(1)} %broadcast_select_fusion), channel_id=1, source_target_pairs={{0,4},{4,0},{8,12},{12,8},{16,20},{20,16},{24,28},{28,24},{1,5},{5... | collective-permute-start | bytes 56 | tf_op jit(solution)/shard_map/ppermute | solution.py:256
  9.4 1.5 %gather_fusion = bf16[4,48,256]{2,1,0:T(8,128)(2,1)S(1)} fusion(bf16[16,48,256]{2,1,0:T(8,128)(2,1)} %param.12, s32[1024]{0:T(1024)S(1)} %pad_clamp_fusion.2), kind=kCustom, calls=%fused_computation | custom fusion | bytes 196624 | tf_op jit(solution)/shard_map/jit(_take)/gather | solution.py:297
  11.0 0.3 collective-permute-start
  11.3 0.7 convert_element_type.99
  12.1 0.8 rev.3
  12.9 0.8 copy.34
  14.2 1.6 %collective-permute-done = bf16[4,48,256]{2,1,0:T(8,128)(2,1)S(1)} collective-permute-done((bf16[4,48,256]{2,1,0:T(8,128)(2,1)S(1)}, bf16[4,48,256]{2,1,0:T(8,128)(2,1)S(1)}, u32[]{:S(2)}, u32[]{:S(2)}) %collective-permute-start) | collective-permute-done | bytes 98336 | tf_op jit(solution)/shard_map/ppermute | solution.py:256
  15.9 1.2 %gather_fusion.1 = bf16[8,48,256]{2,1,0:T(8,128)(2,1)} fusion(bf16[20,48,256]{2,1,0:T(8,128)(2,1)S(1)} %pad_maximum_fusion, s32[1024]{0:T(1024)S(1)} %pad_clamp_fusion.1), kind=kCustom, calls=%fused_computation.1 | custom fusion | bytes 393248 | tf_op jit(solution)/shard_map/jit(_take)/gather | solution.py:306
  17.1 12.1 %exchange.2.pieces = bf16[56,48,256]{2,1,0:T(8,128)(2,1)} custom-call(bf16[8,48,256]{2,1,0:T(8,128)(2,1)} %gather_fusion.1), custom_call_target="tpu_custom_call" | custom-call | bytes 40000000 | tf_op jit(solution)/shard_map/exchange/pallas_call | solution.py:262
  29.2 1.3 %copy-done.2 = bf16[56,48,256]{2,1,0:T(8,128)(2,1)S(1)} copy-done((bf16[56,48,256]{2,1,0:T(8,128)(2,1)S(1)}, bf16[56,48,256]{2,1,0:T(8,128)(2,1)}, u32[]{:S(2)}) %copy-start.2) | copy-done | bytes 1376280
  30.6 4.8 %forward_conv.1 = (bf16[384,256]{1,0:T(8,128)(2,1)S(1)}, bf16[544,384]{1,0:T(8,128)(2,1)S(1)}) custom-call(s32[8,8]{1,0:T(8,128)S(1)} %and_select_fusion.ids, bf16[56,48,256]{2,1,0:T(8,128)(2,1)S(1)} %copy-done.2, bf16[544,1024]{1,0:T(8,128)(2,1)S(1)} %copy-done.3, f32[49,384]{1,0:T(8,128)S(1)} %tile.9.weights), custom_call_target="tpu_custom_call" | custom-call | tf_op jit(solution)/shard_map/forward_conv/pallas_call | solution.py:343
  35.5 1.6 %collective-permute-start.3 = (bf16[8,48,256]{2,1,0:T(8,128)(2,1)S(1)}, bf16[8,48,256]{2,1,0:T(8,128)(2,1)}, u32[]{:S(2)}, u32[]{:S(2)}) collective-permute-start(bf16[8,48,256]{2,1,0:T(8,128)(2,1)S(1)} %bitcast.59), channel_id=1, source_target_pairs={{0,2},{1,3},{2,0},{3,1},{4,6},{5,7},{6,4},{7,5},{8,10},{9,11},{10,... | collective-permute-start | bytes 589832 | tf_op jit(solution)/shard_map/ppermute | solution.py:256
  37.1 0.3 collective-permute-start.4
  37.4 0.6 gather_fusion.3
  38.0 0.6 gather_fusion.2
  38.9 0.7 tile.20
  39.7 1.0 tile.21.weights
  40.8 2.6 %collective-permute-done.3.m2 = bf16[8,48,256]{2,1,0:T(8,128)(2,1)} collective-permute-done((bf16[8,48,256]{2,1,0:T(8,128)(2,1)S(1)}, bf16[8,48,256]{2,1,0:T(8,128)(2,1)}, u32[]{:S(2)}, u32[]{:S(2)}) %collective-permute-start.3) | collective-permute-done | bytes 196640 | tf_op jit(solution)/shard_map/ppermute | solution.py:256
  43.4 3.3 %collective-permute-done.4.m3 = bf16[8,48,256]{2,1,0:T(8,128)(2,1)} collective-permute-done((bf16[8,48,256]{2,1,0:T(8,128)(2,1)S(1)}, bf16[8,48,256]{2,1,0:T(8,128)(2,1)}, u32[]{:S(2)}, u32[]{:S(2)}) %collective-permute-start.4) | collective-permute-done | bytes 196640 | tf_op jit(solution)/shard_map/ppermute | solution.py:256
  46.7 4.4 %mlp.1 = (bf16[4,8,48,256]{3,2,1,0:T(8,128)(2,1)S(1)}, bf16[4,9,48,256]{3,2,1,0:T(8,128)(2,1)S(1)}, bf16[8,48,192]{2,1,0:T(8,128)(2,1)S(1)}, f32[2,8,256]{2,1,0:T(8,128)S(1)}) custom-call(s32[4]{0:T(128)S(1)} %iota_xor_fusion.perm, bf16[8,48,256]{2,1,0:T(8,128)(2,1)S(1)} %bitcast.61, bf16[8,48,256]{2,1,0:T(8,128)(2,1)S(1)} %collective-permute-done.2.m1, ...), custom_call_target="tpu_custom_call" | custom-call | tf_op jit(solution)/shard_map/mlp/pallas_call | solution.py:359
  51.1 2.5 %collective-permute-start.17 = (bf16[8,48,192]{2,1,0:T(8,128)(2,1)S(1)}, bf16[8,48,192]{2,1,0:T(8,128)(2,1)S(1)}, u32[]{:S(2)}, u32[]{:S(2)}) collective-permute-start(bf16[8,48,192]{2,1,0:T(8,128)(2,1)S(1)} %get-tuple-element.16), channel_id=1, source_target_pairs={{0,4},{4,0},{8,12},{12,8},{16,20},{20,16},{24,28},{28,24},{1,5},{5... | collective-permute-start | bytes 442376 | tf_op jit(solution)/shard_map/ppermute | solution.py:256
  53.8 1.6 %collective-permute-start.12 = (bf16[9,48,256]{2,1,0:T(8,128)(2,1)S(1)}, bf16[9,48,256]{2,1,0:T(8,128)(2,1)S(1)}, u32[]{:S(2)}, u32[]{:S(2)}) collective-permute-start(bf16[9,48,256]{2,1,0:T(8,128)(2,1)S(1)} %get-tuple-element.42), channel_id=1, source_target_pairs={{0,2},{1,3},{2,0},{3,1},{4,6},{5,7},{6,4},{7,5},{8,10},{9,11},{10,... | collective-permute-start | bytes 663560 | tf_op jit(solution)/shard_map/ppermute | solution.py:256
  55.3 0.3 collective-permute-start.13
  55.7 1.5 %collective-permute-start.10 = (bf16[8,48,256]{2,1,0:T(8,128)(2,1)S(1)}, bf16[8,48,256]{2,1,0:T(8,128)(2,1)S(1)}, u32[]{:S(2)}, u32[]{:S(2)}) collective-permute-start(bf16[8,48,256]{2,1,0:T(8,128)(2,1)S(1)} %get-tuple-element.44), channel_id=1, source_target_pairs={{0,3},{1,2},{2,1},{3,0},{4,7},{5,6},{6,5},{7,4},{8,11},{9,10},{10,... | collective-permute-start | bytes 589832 | tf_op jit(solution)/shard_map/ppermute | solution.py:256
  57.4 4.7 %collective-permute-done.12 = bf16[9,48,256]{2,1,0:T(8,128)(2,1)S(1)} collective-permute-done((bf16[9,48,256]{2,1,0:T(8,128)(2,1)S(1)}, bf16[9,48,256]{2,1,0:T(8,128)(2,1)S(1)}, u32[]{:S(2)}, u32[]{:S(2)}) %collective-permute-start.12) | collective-permute-done | bytes 221216 | tf_op jit(solution)/shard_map/ppermute | solution.py:256
  62.1 1.5 %collective-permute-start.9 = (bf16[8,48,256]{2,1,0:T(8,128)(2,1)S(1)}, bf16[8,48,256]{2,1,0:T(8,128)(2,1)S(1)}, u32[]{:S(2)}, u32[]{:S(2)}) collective-permute-start(bf16[8,48,256]{2,1,0:T(8,128)(2,1)S(1)} %get-tuple-element.45), channel_id=1, source_target_pairs={{0,2},{1,3},{2,0},{3,1},{4,6},{5,7},{6,4},{7,5},{8,10},{9,11},{10,... | collective-permute-start | bytes 589832 | tf_op jit(solution)/shard_map/ppermute | solution.py:256
  63.5 2.3 %collective-permute-done.13 = bf16[9,48,256]{2,1,0:T(8,128)(2,1)S(1)} collective-permute-done((bf16[9,48,256]{2,1,0:T(8,128)(2,1)S(1)}, bf16[9,48,256]{2,1,0:T(8,128)(2,1)S(1)}, u32[]{:S(2)}, u32[]{:S(2)}) %collective-permute-start.13) | collective-permute-done | bytes 221216 | tf_op jit(solution)/shard_map/ppermute | solution.py:256
  66.2 3.2 %kernel_grad.1 = f32[56,48]{1,0:T(8,128)S(1)} custom-call(bf16[384,256]{1,0:T(8,128)(2,1)S(1)} %bitcast.52, bf16[544,384]{1,0:T(8,128)(2,1)S(1)} %get-tuple-element.15.padded, f32[384,48]{1,0:T(8,128)S(1)} %copy-done.6), custom_call_target="tpu_custom_call" | custom-call | tf_op jit(solution)/shard_map/kernel_grad/pallas_call | solution.py:387
  69.5 0.2 collective-permute-start.14
  69.8 3.8 %collective-permute-start.18 = (bf16[8,48,192]{2,1,0:T(8,128)(2,1)S(1)}, bf16[8,48,192]{2,1,0:T(8,128)(2,1)S(1)}, u32[]{:S(2)}, u32[]{:S(2)}) collective-permute-start(bf16[8,48,192]{2,1,0:T(8,128)(2,1)S(1)} %reduce-precision_convert_fusion.1), channel_id=1, source_target_pairs={{0,8},{4,12},{8,0},{12,4},{16,24},{20,28},{24,16},{28,20},{1,9},{5... | collective-permute-start | bytes 442376 | tf_op jit(solution)/shard_map/ppermute | solution.py:256
  73.7 3.6 %collective-permute-start.15 = (f32[56,48]{1,0:T(8,128)S(1)}, f32[56,48]{1,0:T(8,128)S(1)}, u32[]{:S(2)}, u32[]{:S(2)}) collective-permute-start(f32[56,48]{1,0:T(8,128)S(1)} %add.99), channel_id=1, source_target_pairs={{0,8},{4,12},{8,0},{12,4},{16,24},{20,28},{24,16},{28,20},{1,9},{5... | collective-permute-start | bytes 32264 | tf_op jit(solution)/shard_map/ppermute | solution.py:256
  77.3 0.8 add_convert_fusion
  78.1 11.9 %exchange.3.pieces = bf16[56,48,256]{2,1,0:T(8,128)(2,1)} custom-call(bf16[8,48,256]{2,1,0:T(8,128)(2,1)} %copy-done.4), custom_call_target="tpu_custom_call" | custom-call | bytes 40000000 | tf_op jit(solution)/shard_map/exchange/pallas_call | solution.py:262
  90.0 1.3 %copy-done.1 = bf16[56,48,256]{2,1,0:T(8,128)(2,1)S(1)} copy-done((bf16[56,48,256]{2,1,0:T(8,128)(2,1)S(1)}, bf16[56,48,256]{2,1,0:T(8,128)(2,1)}, u32[]{:S(2)}) %copy-start.1) | copy-done | bytes 1376280
  91.3 5.5 %backward_conv.1 = bf16[384,256]{1,0:T(8,128)(2,1)} custom-call(s32[8,8]{1,0:T(8,128)S(1)} %and_select_fusion.ids, bf16[56,48,256]{2,1,0:T(8,128)(2,1)S(1)} %copy-done.1, bf16[544,1024]{1,0:T(8,128)(2,1)S(1)} %copy-done.3, f32[49,384]{1,0:T(8,128)S(1)} %tile.21.weights, bf16[384,256]{1,0:T(8,128)(2,1)S(1)} %bitcast.57), custom_call_target="tpu_custom_call" | custom-call | tf_op jit(solution)/shard_map/backward_conv/pallas_call | solution.py:416
  96.9 6.3 %collective-permute-start.16 = (f32[56,48]{1,0:T(8,128)S(1)}, f32[56,48]{1,0:T(8,128)S(1)}, u32[]{:S(2)}, u32[]{:S(2)}) collective-permute-start(f32[56,48]{1,0:T(8,128)S(1)} %add.100), channel_id=1, source_target_pairs={{0,16},{4,20},{8,24},{12,28},{16,0},{20,4},{24,8},{28,12},{1,17},{... | collective-permute-start | bytes 32264 | tf_op jit(solution)/shard_map/ppermute | solution.py:256
  103.3 5.5 %collective-permute-done.16 = f32[56,48]{1,0:T(8,128)S(1)} collective-permute-done((f32[56,48]{1,0:T(8,128)S(1)}, f32[56,48]{1,0:T(8,128)S(1)}, u32[]{:S(2)}, u32[]{:S(2)}) %collective-permute-start.16) | collective-permute-done | bytes 10784 | tf_op jit(solution)/shard_map/ppermute | solution.py:256
  108.9 0.7 copy.41
  109.6 3.4 %collective-permute-done.19 = bf16[8,48,192]{2,1,0:T(8,128)(2,1)S(1)} collective-permute-done((bf16[8,48,192]{2,1,0:T(8,128)(2,1)S(1)}, bf16[8,48,192]{2,1,0:T(8,128)(2,1)S(1)}, u32[]{:S(2)}, u32[]{:S(2)}) %collective-permute-start.19) | collective-permute-done | bytes 147488 | tf_op jit(solution)/shard_map/ppermute | solution.py:256
  113.0 0.7 slice_multiply_fusion.1
  113.7 0.8 copy.40
  (81 shorter events, 2.6 us)
Async XLA Ops:
  0.6 37.4 %copy-start = (bf16[192,192]{1,0:T(8,128)(2,1)S(1)}, bf16[192,192]{1,0:T(8,128)(2,1)}, u32[]{:S(2)}) copy-start(bf16[192,192]{1,0:T(8,128)(2,1)} %param.18) | copy-start | bytes 221188
  0.6 15.2 %copy-start.8 = (bf16[16,48,256]{2,1,0:T(8,128)(2,1)S(1)}, bf16[16,48,256]{2,1,0:T(8,128)(2,1)}, u32[]{:S(2)}) copy-start(bf16[16,48,256]{2,1,0:T(8,128)(2,1)} %param.12) | copy-start | bytes 1179652
  0.7 13.3 %copy-start.9 = (bf16[192,192]{1,0:T(8,128)(2,1)S(1)}, bf16[192,192]{1,0:T(8,128)(2,1)}, u32[]{:S(2)}) copy-start(bf16[192,192]{1,0:T(8,128)(2,1)} %param.20) | copy-start | bytes 221188
  0.7 13.4 %copy-start.10 = (s32[8,8]{1,0:T(8,128)S(1)}, s32[8,8]{1,0:T(8,128)}, u32[]{:S(2)}) copy-start(s32[8,8]{1,0:T(8,128)} %param.14) | copy-start | bytes 772
  2.5 34.5 %collective-permute-start.5 = (bf16[9,48,256]{2,1,0:T(8,128)(2,1)S(1)}, bf16[9,48,256]{2,1,0:T(8,128)(2,1)S(1)}, u32[]{:S(2)}, u32[]{:S(2)}) collective-permute-start(bf16[9,48,256]{2,1,0:T(8,128)(2,1)S(1)} %pad_maximum_fusion.1.d0), channel_id=1, source_target_pairs={{0,1},{1,0},{2,3},{3,2},{4,5},{5,4},{6,7},{7,6},{8,9},{9,8},{10,11... | collective-permute-start | bytes 663560 | tf_op jit(solution)/shard_map/ppermute | solution.py:256
  3.0 37.7 %collective-permute-start.6 = (bf16[9,48,256]{2,1,0:T(8,128)(2,1)S(1)}, bf16[9,48,256]{2,1,0:T(8,128)(2,1)S(1)}, u32[]{:S(2)}, u32[]{:S(2)}) collective-permute-start(bf16[9,48,256]{2,1,0:T(8,128)(2,1)S(1)} %pad_maximum_fusion.1.d0), channel_id=1, source_target_pairs={{0,2},{1,3},{2,0},{3,1},{4,6},{5,7},{6,4},{7,5},{8,10},{9,11},{10,... | collective-permute-start | bytes 663560 | tf_op jit(solution)/shard_map/ppermute | solution.py:256
  5.6 35.1 %collective-permute-start.7 = (bf16[9,48,256]{2,1,0:T(8,128)(2,1)S(1)}, bf16[9,48,256]{2,1,0:T(8,128)(2,1)S(1)}, u32[]{:S(2)}, u32[]{:S(2)}) collective-permute-start(bf16[9,48,256]{2,1,0:T(8,128)(2,1)S(1)} %pad_maximum_fusion.1.d0), channel_id=1, source_target_pairs={{0,3},{1,2},{2,1},{3,0},{4,7},{5,6},{6,5},{7,4},{8,11},{9,10},{10,... | collective-permute-start | bytes 663560 | tf_op jit(solution)/shard_map/ppermute | solution.py:256
  7.6 6.4 %collective-permute-start.1 = (s32[4]{0:T(128)S(1)}, s32[4]{0:T(128)S(1)}, u32[]{:S(2)}, u32[]{:S(2)}) collective-permute-start(s32[4]{0:T(128)S(1)} %broadcast_select_fusion), channel_id=1, source_target_pairs={{0,4},{4,0},{8,12},{12,8},{16,20},{20,16},{24,28},{28,24},{1,5},{5... | collective-permute-start | bytes 56 | tf_op jit(solution)/shard_map/ppermute | solution.py:256
  11.0 4.8 %collective-permute-start = (bf16[4,48,256]{2,1,0:T(8,128)(2,1)S(1)}, bf16[4,48,256]{2,1,0:T(8,128)(2,1)S(1)}, u32[]{:S(2)}, u32[]{:S(2)}) collective-permute-start(bf16[4,48,256]{2,1,0:T(8,128)(2,1)S(1)} %gather_fusion), channel_id=1, source_target_pairs={{0,4},{4,0},{8,12},{12,8},{16,20},{20,16},{24,28},{28,24},{1,5},{5... | collective-permute-start | bytes 294920 | tf_op jit(solution)/shard_map/ppermute | solution.py:256
  14.2 15.1 %copy-start.3 = (bf16[544,1024]{1,0:T(8,128)(2,1)S(1)}, bf16[544,1024]{1,0:T(8,128)(2,1)}, u32[]{:S(2)}) copy-start(bf16[544,1024]{1,0:T(8,128)(2,1)} %constant.68.clone.place) | copy-start | bytes 3342340
  29.2 1.3 %copy-start.2 = (bf16[56,48,256]{2,1,0:T(8,128)(2,1)S(1)}, bf16[56,48,256]{2,1,0:T(8,128)(2,1)}, u32[]{:S(2)}) copy-start(bf16[56,48,256]{2,1,0:T(8,128)(2,1)} %exchange.2.pieces) | copy-start | bytes 4128772
  30.6 8.1 %copy-start.12 = (bf16[192]{0:T(256)(128)(2,1)S(1)}, bf16[192]{0:T(256)(128)(2,1)}, u32[]{:S(2)}) copy-start(bf16[192]{0:T(256)(128)(2,1)} %param.19) | copy-start | bytes 1156
  35.4 5.3 %collective-permute-start.2 = (bf16[8,48,256]{2,1,0:T(8,128)(2,1)S(1)}, bf16[8,48,256]{2,1,0:T(8,128)(2,1)S(1)}, u32[]{:S(2)}, u32[]{:S(2)}) collective-permute-start(bf16[8,48,256]{2,1,0:T(8,128)(2,1)S(1)} %bitcast.58), channel_id=1, source_target_pairs={{0,1},{1,0},{2,3},{3,2},{4,5},{5,4},{6,7},{7,6},{8,9},{9,8},{10,11... | collective-permute-start | bytes 589832 | tf_op jit(solution)/shard_map/ppermute | solution.py:256
  35.5 7.9 %collective-permute-start.3 = (bf16[8,48,256]{2,1,0:T(8,128)(2,1)S(1)}, bf16[8,48,256]{2,1,0:T(8,128)(2,1)}, u32[]{:S(2)}, u32[]{:S(2)}) collective-permute-start(bf16[8,48,256]{2,1,0:T(8,128)(2,1)S(1)} %bitcast.59), channel_id=1, source_target_pairs={{0,2},{1,3},{2,0},{3,1},{4,6},{5,7},{6,4},{7,5},{8,10},{9,11},{10,... | collective-permute-start | bytes 589832 | tf_op jit(solution)/shard_map/ppermute | solution.py:256
  37.1 9.6 %collective-permute-start.4 = (bf16[8,48,256]{2,1,0:T(8,128)(2,1)S(1)}, bf16[8,48,256]{2,1,0:T(8,128)(2,1)}, u32[]{:S(2)}, u32[]{:S(2)}) collective-permute-start(bf16[8,48,256]{2,1,0:T(8,128)(2,1)S(1)} %bitcast.60), channel_id=1, source_target_pairs={{0,3},{1,2},{2,1},{3,0},{4,7},{5,6},{6,5},{7,4},{8,11},{9,10},{10,... | collective-permute-start | bytes 589832 | tf_op jit(solution)/shard_map/ppermute | solution.py:256
  51.1 18.6 %collective-permute-start.17 = (bf16[8,48,192]{2,1,0:T(8,128)(2,1)S(1)}, bf16[8,48,192]{2,1,0:T(8,128)(2,1)S(1)}, u32[]{:S(2)}, u32[]{:S(2)}) collective-permute-start(bf16[8,48,192]{2,1,0:T(8,128)(2,1)S(1)} %get-tuple-element.16), channel_id=1, source_target_pairs={{0,4},{4,0},{8,12},{12,8},{16,20},{20,16},{24,28},{28,24},{1,5},{5... | collective-permute-start | bytes 442376 | tf_op jit(solution)/shard_map/ppermute | solution.py:256
  53.7 3.5 %collective-permute-start.11 = (bf16[9,48,256]{2,1,0:T(8,128)(2,1)S(1)}, bf16[9,48,256]{2,1,0:T(8,128)(2,1)S(1)}, u32[]{:S(2)}, u32[]{:S(2)}) collective-permute-start(bf16[9,48,256]{2,1,0:T(8,128)(2,1)S(1)} %get-tuple-element.40), channel_id=1, source_target_pairs={{0,1},{1,0},{2,3},{3,2},{4,5},{5,4},{6,7},{7,6},{8,9},{9,8},{10,11... | collective-permute-start | bytes 663560 | tf_op jit(solution)/shard_map/ppermute | solution.py:256
  53.8 8.3 %collective-permute-start.12 = (bf16[9,48,256]{2,1,0:T(8,128)(2,1)S(1)}, bf16[9,48,256]{2,1,0:T(8,128)(2,1)S(1)}, u32[]{:S(2)}, u32[]{:S(2)}) collective-permute-start(bf16[9,48,256]{2,1,0:T(8,128)(2,1)S(1)} %get-tuple-element.42), channel_id=1, source_target_pairs={{0,2},{1,3},{2,0},{3,1},{4,6},{5,7},{6,4},{7,5},{8,10},{9,11},{10,... | collective-permute-start | bytes 663560 | tf_op jit(solution)/shard_map/ppermute | solution.py:256
  55.3 10.6 %collective-permute-start.13 = (bf16[9,48,256]{2,1,0:T(8,128)(2,1)S(1)}, bf16[9,48,256]{2,1,0:T(8,128)(2,1)S(1)}, u32[]{:S(2)}, u32[]{:S(2)}) collective-permute-start(bf16[9,48,256]{2,1,0:T(8,128)(2,1)S(1)} %get-tuple-element.41), channel_id=1, source_target_pairs={{0,3},{1,2},{2,1},{3,0},{4,7},{5,6},{6,5},{7,4},{8,11},{9,10},{10,... | collective-permute-start | bytes 663560 | tf_op jit(solution)/shard_map/ppermute | solution.py:256
  55.7 10.5 %copy-start.6 = (f32[384,48]{1,0:T(8,128)S(1)}, f32[384,48]{1,0:T(8,128)}, u32[]{:S(2)}) copy-start(f32[384,48]{1,0:T(8,128)} %constant.69.clone.fold) | copy-start | bytes 221188
  55.7 21.5 %collective-permute-start.10 = (bf16[8,48,256]{2,1,0:T(8,128)(2,1)S(1)}, bf16[8,48,256]{2,1,0:T(8,128)(2,1)S(1)}, u32[]{:S(2)}, u32[]{:S(2)}) collective-permute-start(bf16[8,48,256]{2,1,0:T(8,128)(2,1)S(1)} %get-tuple-element.44), channel_id=1, source_target_pairs={{0,3},{1,2},{2,1},{3,0},{4,7},{5,6},{6,5},{7,4},{8,11},{9,10},{10,... | collective-permute-start | bytes 589832 | tf_op jit(solution)/shard_map/ppermute | solution.py:256
  57.2 20.0 %collective-permute-start.8 = (bf16[8,48,256]{2,1,0:T(8,128)(2,1)S(1)}, bf16[8,48,256]{2,1,0:T(8,128)(2,1)S(1)}, u32[]{:S(2)}, u32[]{:S(2)}) collective-permute-start(bf16[8,48,256]{2,1,0:T(8,128)(2,1)S(1)} %get-tuple-element.43), channel_id=1, source_target_pairs={{0,1},{1,0},{2,3},{3,2},{4,5},{5,4},{6,7},{7,6},{8,9},{9,8},{10,11... | collective-permute-start | bytes 589832 | tf_op jit(solution)/shard_map/ppermute | solution.py:256
  62.1 15.2 %collective-permute-start.9 = (bf16[8,48,256]{2,1,0:T(8,128)(2,1)S(1)}, bf16[8,48,256]{2,1,0:T(8,128)(2,1)S(1)}, u32[]{:S(2)}, u32[]{:S(2)}) collective-permute-start(bf16[8,48,256]{2,1,0:T(8,128)(2,1)S(1)} %get-tuple-element.45), channel_id=1, source_target_pairs={{0,2},{1,3},{2,0},{3,1},{4,6},{5,7},{6,4},{7,5},{8,10},{9,11},{10,... | collective-permute-start | bytes 589832 | tf_op jit(solution)/shard_map/ppermute | solution.py:256
  66.0 11.2 %copy-start.7 = (bf16[8,48,256]{2,1,0:T(8,128)(2,1)S(1)}, bf16[8,48,256]{2,1,0:T(8,128)(2,1)}, u32[]{:S(2)}) copy-start(bf16[8,48,256]{2,1,0:T(8,128)(2,1)} %gather_fusion.1) | copy-start | bytes 589828
  66.0 11.2 %copy-start.11 = (f32[48]{0:T(128)S(1)}, f32[48]{0:T(128)}, u32[]{:S(2)}) copy-start(f32[48]{0:T(128)} %param.21) | copy-start | bytes 580
  66.2 11.9 %copy-start.4 = (bf16[8,48,256]{2,1,0:T(8,128)(2,1)}, bf16[8,48,256]{2,1,0:T(8,128)(2,1)S(1)}, u32[]{:S(2)}) copy-start(bf16[8,48,256]{2,1,0:T(8,128)(2,1)S(1)} %fusion.3.own) | copy-start | bytes 589828
  69.5 4.2 %collective-permute-start.14 = (f32[56,48]{1,0:T(8,128)S(1)}, f32[56,48]{1,0:T(8,128)S(1)}, u32[]{:S(2)}, u32[]{:S(2)}) collective-permute-start(f32[56,48]{1,0:T(8,128)S(1)} %kernel_grad.1), channel_id=1, source_target_pairs={{0,4},{4,0},{8,12},{12,8},{16,20},{20,16},{24,28},{28,24},{1,5},{5... | collective-permute-start | bytes 32264 | tf_op jit(solution)/shard_map/ppermute | solution.py:256
  69.8 33.4 %collective-permute-start.18 = (bf16[8,48,192]{2,1,0:T(8,128)(2,1)S(1)}, bf16[8,48,192]{2,1,0:T(8,128)(2,1)S(1)}, u32[]{:S(2)}, u32[]{:S(2)}) collective-permute-start(bf16[8,48,192]{2,1,0:T(8,128)(2,1)S(1)} %reduce-precision_convert_fusion.1), channel_id=1, source_target_pairs={{0,8},{4,12},{8,0},{12,4},{16,24},{20,28},{24,16},{28,20},{1,9},{5... | collective-permute-start | bytes 442376 | tf_op jit(solution)/shard_map/ppermute | solution.py:256
  73.7 16.3 %copy-start.5 = (bf16[8,48,256]{2,1,0:T(8,128)(2,1)S(1)}, bf16[8,48,256]{2,1,0:T(8,128)(2,1)}, u32[]{:S(2)}) copy-start(bf16[8,48,256]{2,1,0:T(8,128)(2,1)} %param.15) | copy-start | bytes 589828
  73.7 23.2 %collective-permute-start.15 = (f32[56,48]{1,0:T(8,128)S(1)}, f32[56,48]{1,0:T(8,128)S(1)}, u32[]{:S(2)}, u32[]{:S(2)}) collective-permute-start(f32[56,48]{1,0:T(8,128)S(1)} %add.99), channel_id=1, source_target_pairs={{0,8},{4,12},{8,0},{12,4},{16,24},{20,28},{24,16},{28,20},{1,9},{5... | collective-permute-start | bytes 32264 | tf_op jit(solution)/shard_map/ppermute | solution.py:256
  90.0 1.3 %copy-start.1 = (bf16[56,48,256]{2,1,0:T(8,128)(2,1)S(1)}, bf16[56,48,256]{2,1,0:T(8,128)(2,1)}, u32[]{:S(2)}) copy-start(bf16[56,48,256]{2,1,0:T(8,128)(2,1)} %exchange.3.pieces) | copy-start | bytes 4128772
  96.9 12.0 %collective-permute-start.16 = (f32[56,48]{1,0:T(8,128)S(1)}, f32[56,48]{1,0:T(8,128)S(1)}, u32[]{:S(2)}, u32[]{:S(2)}) collective-permute-start(f32[56,48]{1,0:T(8,128)S(1)} %add.100), channel_id=1, source_target_pairs={{0,16},{4,20},{8,24},{12,28},{16,0},{20,4},{24,8},{28,12},{1,17},{... | collective-permute-start | bytes 32264 | tf_op jit(solution)/shard_map/ppermute | solution.py:256
  103.3 9.7 %collective-permute-start.19 = (bf16[8,48,192]{2,1,0:T(8,128)(2,1)S(1)}, bf16[8,48,192]{2,1,0:T(8,128)(2,1)S(1)}, u32[]{:S(2)}, u32[]{:S(2)}) collective-permute-start(bf16[8,48,192]{2,1,0:T(8,128)(2,1)S(1)} %reduce-precision_convert_fusion), channel_id=1, source_target_pairs={{0,16},{4,20},{8,24},{12,28},{16,0},{20,4},{24,8},{28,12},{1,17},{... | collective-permute-start | bytes 442376 | tf_op jit(solution)/shard_map/ppermute | solution.py:256
